TPU v7x, 128 devices: a whole 4x4x4 slice. The times are simulated.
128 devices in a mesh: seq: 64 (over y, x, z), batch: 2 (over core).
Axes of the slice: x: 4, y: 4, z: 4, core: 2. Of those that a mesh axis runs over, the one named last changes fastest.
Arguments:
- queries: bfloat16 [2, 32768, 2048], P('batch', 'seq'), may hold values from -24 to 24
- key_vectors: bfloat16 [2, 32768, 2048], P('batch', 'seq'), may hold values from -24 to 24
- values: bfloat16 [2, 32768, 2048], P('batch', 'seq'), may hold values from -8 to 8
- out_grad: bfloat16 [2, 32768, 2048], P('batch', 'seq'), may hold values from -36 to 36
- far_lists: int32 [2, 64, 12], P('batch'), may hold values from 0 to 63, as said below
- level_bias: float32 [3, 16], replicated, may hold values from -1.5 to 1.5
Outputs:
- attended: bfloat16 [2, 32768, 2048], P('batch', 'seq')
- query_grad: bfloat16 [2, 32768, 2048], P('batch', 'seq')
- key_grad: bfloat16 [2, 32768, 2048], P('batch', 'seq')
- value_grad: bfloat16 [2, 32768, 2048], P('batch', 'seq')
- level_grad: float32 [3, 16], replicated
Inputs may be any that keep to these rules, and one draw needn't show every extreme that they name: Every row far_lists[b, i] holds 12 different block numbers, none of them i - 1, i or i + 1.
All inputs are finite; a program needn't handle non-finite values.
Results may differ from a plain program's by a relative error of at most 0.024.
Values may be sent and summed in bfloat16 or wider, within the bound.
A program may use at most 192 MiB of HBM per device.

v0:
```python
import math

import jax
import jax.numpy as jnp
from jax import lax
from jax.sharding import PartitionSpec as P

RIM = 256
TOP_ROWS = 4
SLOTS = 4


NEG_FILL = -1e30


def with_halo(cells, sides, width):
    for axis, dim in sides:
        count = lax.axis_size(axis)
        ends = count - 1
        head = lax.slice_in_dim(cells, 0, width, axis=dim)
        tail = lax.slice_in_dim(cells, cells.shape[dim] - width, cells.shape[dim], axis=dim)
        cells = jnp.concatenate(
            [
                lax.ppermute(tail, axis, [(i, (i + 1) % count) for i in range(ends)]),
                cells,
                lax.ppermute(head, axis, [((i + 1) % count, i) for i in range(ends)]),
            ],
            axis=dim,
        )
    return cells


def shifted(value, axis, steps):
    count = lax.axis_size(axis)
    initial, last = (max(0, -steps), min(count, count - steps))
    return lax.ppermute(value, axis, [(source, source + steps) for source in range(initial, last)])


def level_layout(top_rows):
    counts = [top_rows, top_rows // 2, top_rows // 4]
    offsets = [0, top_rows, top_rows + top_rows // 2]
    return (counts, offsets)


def pooled_rows(tokens, top_rows):
    length, feature_width = tokens.shape
    widened = tokens.astype(jnp.float32)
    counts, offsets = level_layout(top_rows)
    pieces = [
        jnp.mean(widened.reshape(row_count, length // row_count, feature_width), axis=1)
        for row_count in counts
    ]
    return jnp.concatenate(pieces, axis=0)


def far_bias(level_bias, top_rows, slot_count, leaf_len):
    counts, offsets = level_layout(top_rows)
    columns = []
    for level_no in range(3):
        lifted = level_bias[level_no] + math.log(leaf_len // counts[level_no])
        columns.append(jnp.repeat(lifted[:, None], slot_count * counts[level_no], axis=1))
    return jnp.concatenate(columns, axis=1)


def far_from_table(summary_table, own_list, offsets, counts, slot_count):
    pieces = []
    for level_no in range(3):
        chosen = own_list[level_no * slot_count : (level_no + 1) * slot_count]
        first_row = offsets[level_no]
        picked = summary_table[chosen][:, :, first_row : first_row + counts[level_no]]
        pieces.append(
            jnp.moveaxis(picked, 0, 1).reshape(
                2, slot_count * counts[level_no], summary_table.shape[-1]
            )
        )
    return jnp.concatenate(pieces, axis=1)


def attend_group(packed, score_scale):
    queries, all_keys, all_values, out_grad, key_bias = packed
    scores = (
        jnp.einsum("qge,kge->gqk", queries, all_keys, preferred_element_type=jnp.float32)
        * score_scale
        + key_bias[:, None, :]
    )
    row_max = jnp.max(scores, axis=-1, keepdims=True)
    raised = jnp.exp(scores - row_max)
    weights = raised / jnp.sum(raised, axis=-1, keepdims=True)
    weights_low = weights.astype(jnp.bfloat16)
    attended = jnp.einsum(
        "gqk,kge->qge", weights_low, all_values, preferred_element_type=jnp.float32
    ).astype(jnp.bfloat16)
    dweights = jnp.einsum("qge,kge->gqk", out_grad, all_values, preferred_element_type=jnp.float32)
    row_dot = jnp.einsum("qge,qge->gq", out_grad, attended, preferred_element_type=jnp.float32)
    dscores = weights * (dweights - row_dot[:, :, None])
    dscores_low = dscores.astype(jnp.bfloat16)
    query_grad = (
        jnp.einsum("gqk,kge->qge", dscores_low, all_keys, preferred_element_type=jnp.float32)
        * score_scale
    )
    key_grad = (
        jnp.einsum("gqk,qge->kge", dscores_low, queries, preferred_element_type=jnp.float32)
        * score_scale
    )
    value_grad = jnp.einsum(
        "gqk,qge->kge", weights_low, out_grad, preferred_element_type=jnp.float32
    )
    bias_grad = jnp.sum(dscores, axis=1)
    return (attended, query_grad, key_grad, value_grad, bias_grad)


def attend_heads(queries, all_keys, all_values, out_grad, key_bias, head_count):
    length, feature_width = queries.shape
    head_dim = feature_width // head_count
    group_size = 4
    group_count = head_count // group_size
    score_scale = 1.0 / math.sqrt(head_dim)

    def to_groups(array):
        return jnp.moveaxis(array.reshape(array.shape[0], group_count, group_size, head_dim), 1, 0)

    def from_groups(array):
        return jnp.moveaxis(array, 0, 1).reshape(array.shape[1], feature_width)

    results = lax.map(
        lambda packed: attend_group(packed, score_scale),
        (
            to_groups(queries),
            to_groups(all_keys),
            to_groups(all_values),
            to_groups(out_grad),
            key_bias.reshape(group_count, group_size, key_bias.shape[1]),
        ),
    )
    return (
        from_groups(results[0]),
        from_groups(results[1]),
        from_groups(results[2]),
        from_groups(results[3]),
        results[4].reshape(head_count, key_bias.shape[1]),
    )


def shards(queries, key_vectors, values, out_grad, far_lists, level_bias):
    block_index = lax.axis_index("seq")
    blocks = lax.axis_size("seq")
    leaf_len = queries.shape[1]
    feature_width = queries.shape[2]
    head_count = level_bias.shape[1]
    counts, offsets = level_layout(TOP_ROWS)
    near_len = leaf_len + 2 * RIM
    own_summary = jnp.stack(
        [pooled_rows(key_vectors[0], TOP_ROWS), pooled_rows(values[0], TOP_ROWS)]
    ).astype(jnp.bfloat16)
    paired = jnp.stack([key_vectors[0], values[0]])
    widened = with_halo(paired, (("seq", 1),), RIM)
    list_rows = far_lists[0]
    own_list = lax.dynamic_index_in_dim(list_rows, block_index, 0, keepdims=False)
    summary_table = lax.all_gather(own_summary[None], "seq", axis=0, tiled=True)
    far_pair = far_from_table(summary_table, own_list, offsets, counts, SLOTS)
    positions = block_index * leaf_len - RIM + jnp.arange(near_len, dtype=jnp.int32)
    inside = (positions >= 0) & (positions < blocks * leaf_len)
    near_bias = jnp.where(inside, 0.0, NEG_FILL).astype(jnp.float32)
    key_bias = jnp.concatenate(
        [
            jnp.broadcast_to(near_bias[None, :], (head_count, near_len)),
            far_bias(level_bias, TOP_ROWS, SLOTS, leaf_len),
        ],
        axis=1,
    )
    all_keys = jnp.concatenate([widened[0], far_pair[0]], axis=0)
    all_values = jnp.concatenate([widened[1], far_pair[1]], axis=0)
    attended, query_grad, key_terms, value_terms, bias_terms = attend_heads(
        queries[0], all_keys, all_values, out_grad[0], key_bias, head_count
    )
    upward = jnp.stack(
        [key_terms[RIM + leaf_len : near_len], value_terms[RIM + leaf_len : near_len]]
    )
    from_below = shifted(upward, "seq", 1)
    downward = jnp.stack([key_terms[:RIM], value_terms[:RIM]])
    from_above = shifted(downward, "seq", -1)
    own_terms = jnp.stack([key_terms[RIM : RIM + leaf_len], value_terms[RIM : RIM + leaf_len]])
    own_terms = own_terms.at[:, :RIM].add(from_below).at[:, leaf_len - RIM :].add(from_above)
    far_terms = jnp.stack([key_terms[near_len:], value_terms[near_len:]])
    block_ids = jnp.arange(blocks, dtype=jnp.int32)
    pool_grads = []
    pieces = []
    column = 0
    for level_no in range(3):
        row_count = counts[level_no]
        sources = own_list[level_no * SLOTS : (level_no + 1) * SLOTS]
        selector = (sources[:, None] == block_ids[None, :]).astype(jnp.float32)
        slot_rows = far_terms[:, column : column + SLOTS * row_count].reshape(
            2, SLOTS, row_count, feature_width
        )
        pieces.append(
            jnp.einsum("sn,csrw->ncrw", selector, slot_rows, precision=lax.Precision.HIGHEST)
        )
        column += SLOTS * row_count
    grad_table = jnp.concatenate(pieces, axis=2)
    summed = lax.psum_scatter(grad_table, "seq", scatter_dimension=0, tiled=True)
    for level_no in range(3):
        pool_grads.append(summed[0, :, offsets[level_no] : offsets[level_no] + counts[level_no]])
    for level_no in range(3):
        pool_length = leaf_len // counts[level_no]
        own_terms = own_terms + jnp.repeat(pool_grads[level_no] / pool_length, pool_length, axis=1)
    far_bias_terms = bias_terms[:, near_len:]
    level_parts = []
    column = 0
    for level_no in range(3):
        span = SLOTS * counts[level_no]
        level_parts.append(jnp.sum(far_bias_terms[:, column : column + span], axis=1))
        column += span
    bias_total = lax.psum(jnp.stack(level_parts), ("seq", "batch"))
    level_grad = bias_total / math.sqrt(lax.axis_size("batch") * blocks * leaf_len)
    return (
        attended[None],
        query_grad.astype(jnp.bfloat16)[None],
        own_terms[0].astype(jnp.bfloat16)[None],
        own_terms[1].astype(jnp.bfloat16)[None],
        level_grad,
    )


def solution(mesh):
    placed = (
        P("batch", "seq", None),
        P("batch", "seq", None),
        P("batch", "seq", None),
        P("batch", "seq", None),
        P("batch", None, None),
        P(),
    )
    return jax.shard_map(
        shards,
        mesh=mesh,
        in_specs=placed,
        out_specs=(
            P("batch", "seq", None),
            P("batch", "seq", None),
            P("batch", "seq", None),
            P("batch", "seq", None),
            P(),
        ),
        check_vma=False,
    )
```

profile of v0, /device:TPU:1, one launch (start us, length us, event | category | flops | bytes accessed | tf_op | source)
XLA Modules:
  0.0 591.1 jit_solution(16481293159211589300)
XLA Ops:
  35.4 5.7 collective-permute-start
  51.7 33.3 %collective-permute-done = bf16[2,256,2048]{1,2,0:T(8,128)(2,1)} collective-permute-done((bf16[2,256,2048]{1,2,0:T(8,128)(2,1)}, bf16[2,256,2048]{1,2,0:T(8,128)(2,1)}, u32[]{:S(2)}, u32[]{:S(2)}) %collective-permute-start) | collective-permute-done | bytes 2097184 | tf_op jit(solution)/shard_map/ppermute | solution.py:24
  85.0 5.1 collective-permute-done.1
  97.8 38.4 %all-gather.2.cloned.1.call-done = bf16[64,2,7,2048]{3,1,2,0:T(2,128)(2,1)} async-done(((bf16[1,2,7,2048]{3,1,2,0:T(2,128)(2,1)}), bf16[64,2,7,2048]{3,1,2,0:T(2,128)(2,1)}) %all-gather.2.cloned.1.call-update) | async-done | bytes 3670032 | tf_op jit(solution)/shard_map/all_gather | solution.py:159
  151.5 6.6 %copy.140 = bf16[4,1052,4,128]{3,1,2,0:T(8,128)(2,1)} copy(bf16[4,1052,4,128]{1,3,2,0:T(8,128)(2,1)} %maximum_bitcast_fusion.1) | data formatting | bytes 8617984 | tf_op jit(solution)/shard_map/while | solution.py:125
  163.3 6.7 %copy.138 = bf16[4,1052,4,128]{3,1,2,0:T(8,128)(2,1)} copy(bf16[4,1052,4,128]{1,3,2,0:T(8,128)(2,1)} %maximum_bitcast_fusion) | data formatting | bytes 8617984 | tf_op jit(solution)/shard_map/while | solution.py:125
  170.0 139.1 %while.20 = (s32[]{:T(128)}, bf16[4,512,4,128]{1,3,2,0:T(8,128)(2,1)S(1)}, bf16[4,512,4,128]{1,3,2,0:T(8,128)(2,1)}, f32[4,1052,4,128]{3,1,2,0:T(8,128)}, f32[4,...) while((s32[]{:T(128)}, ...), condition=%wide.region_10.11_spmd, body=%wide.region_6.10_spmd.sunk | while | flops 3335111680 | bytes 135876688 | solution.py:125
  170.2 7.6 %fusion.123 = (f32[4,512]{1,0:T(4,128)S(1)}, f32[4,512,1052]{1,2,0:T(8,128)}) fusion(f32[4,1052]{1,0:T(4,128)S(1)} %dynamic-slice_bitcast_fusion.2, bf16[4,1052,4,128]{3,1,2,0:T(8,128)(2,1)} %get-tuple-element.313, s32[]{:T(128)} %get-tuple-element.293, bf16[4,512,4,128]{1,3,2,0:T(8,128)(2,1)} %get-tuple-element.312), kind=kOutput, calls=%fused_computation.138.clone.1 | convolution fusion | flops 560169984 | bytes 10249664 | tf_op jit(solution)/shard_map/while/body/eval_jaxpr/sub | solution.py:87
  188.8 5.8 fusion.125
  205.0 7.6 %fusion.123 = (f32[4,512]{1,0:T(4,128)S(1)}, f32[4,512,1052]{1,2,0:T(8,128)}) fusion(f32[4,1052]{1,0:T(4,128)S(1)} %dynamic-slice_bitcast_fusion.2, bf16[4,1052,4,128]{3,1,2,0:T(8,128)(2,1)} %get-tuple-element.313, s32[]{:T(128)} %get-tuple-element.293, bf16[4,512,4,128]{1,3,2,0:T(8,128)(2,1)} %get-tuple-element.312), kind=kOutput, calls=%fused_computation.138.clone.1 | convolution fusion | flops 560169984 | bytes 10249664 | tf_op jit(solution)/shard_map/while/body/eval_jaxpr/sub | solution.py:87
  223.6 5.8 fusion.125
  239.7 7.6 %fusion.123 = (f32[4,512]{1,0:T(4,128)S(1)}, f32[4,512,1052]{1,2,0:T(8,128)}) fusion(f32[4,1052]{1,0:T(4,128)S(1)} %dynamic-slice_bitcast_fusion.2, bf16[4,1052,4,128]{3,1,2,0:T(8,128)(2,1)} %get-tuple-element.313, s32[]{:T(128)} %get-tuple-element.293, bf16[4,512,4,128]{1,3,2,0:T(8,128)(2,1)} %get-tuple-element.312), kind=kOutput, calls=%fused_computation.138.clone.1 | convolution fusion | flops 560169984 | bytes 10249664 | tf_op jit(solution)/shard_map/while/body/eval_jaxpr/sub | solution.py:87
  258.3 5.8 fusion.125
  274.3 7.6 %fusion.123 = (f32[4,512]{1,0:T(4,128)S(1)}, f32[4,512,1052]{1,2,0:T(8,128)}) fusion(f32[4,1052]{1,0:T(4,128)S(1)} %dynamic-slice_bitcast_fusion.2, bf16[4,1052,4,128]{3,1,2,0:T(8,128)(2,1)} %get-tuple-element.313, s32[]{:T(128)} %get-tuple-element.293, bf16[4,512,4,128]{1,3,2,0:T(8,128)(2,1)} %get-tuple-element.312), kind=kOutput, calls=%fused_computation.138.clone.1 | convolution fusion | flops 560169984 | bytes 10249664 | tf_op jit(solution)/shard_map/while/body/eval_jaxpr/sub | solution.py:87
  292.9 5.8 fusion.125
  319.8 11.7 %copy.156 = f32[64,2,7,2048]{3,1,2,0:T(2,128)} copy(f32[64,2,7,2048]{3,0,2,1:T(8,128)} %pad_maximum_fusion.1) | data formatting | bytes 14680064 | tf_op jit(solution)/shard_map/concatenate | solution.py:200
  379.4 6.9 %copy.144 = f32[512,4,4,128]{3,2,1,0:T(4,128)} copy(f32[512,4,4,128]{3,0,2,1:T(8,128)} %slice.230) | data formatting | bytes 8388608 | tf_op jit(solution)/shard_map/slice | solution.py:182
  386.2 5.5 stack.64
  391.7 6.9 %copy.145 = f32[512,4,4,128]{3,2,1,0:T(4,128)} copy(f32[512,4,4,128]{3,0,2,1:T(8,128)} %slice.231) | data formatting | bytes 8388608 | tf_op jit(solution)/shard_map/slice | solution.py:182
  398.5 5.6 stack.65
  410.9 113.2 %psum.7 = f32[3,16]{1,0:T(4,128)S(1)} all-reduce(f32[3,16]{1,0:T(4,128)S(1)} %pad_maximum_fusion.7), channel_id=1, replica_groups=mesh['seq'=64,'batch'=2] {'seq','batch'}, use_global_device_ids=true, to_apply=%region_15.16 | all-reduce | flops 48 | bytes 384 | tf_op jit(solution)/shard_map/psum | solution.py:214
  531.9 6.6 %fusion.58 = f32[2,512,2048]{2,1,0:T(8,128)} fusion(f32[2,512,2048]{2,1,0:T(8,128)} %constant_dynamic-update-slice_fusion, f32[2,256,2048]{2,1,0:T(8,128)} %collective-permute-done.2), kind=kLoop, calls=%fused_computation.68 | loop fusion | flops 1048576 | bytes 12582912 | tf_op jit(solution)/shard_map/scatter-add | solution.py:183
  538.5 6.5 %fusion.57 = f32[2,512,2048]{2,1,0:T(8,128)} fusion(f32[2,512,2048]{2,1,0:T(8,128)} %fusion.58, f32[2,256,2048]{2,1,0:T(8,128)} %collective-permute-done.3), kind=kLoop, calls=%fused_computation.66 | loop fusion | flops 1048576 | bytes 12582912 | tf_op jit(solution)/shard_map/scatter-add | solution.py:183
  545.0 27.6 %all-reduce.3.cloned.1.call-done = f32[64,2,7,2048]{3,1,2,0:T(2,128)} async-done(((f32[64,2,7,2048]{3,1,2,0:T(2,128)}), f32[64,2,7,2048]{3,1,2,0:T(2,128)}) %all-reduce.3.cloned.1.call-update) | async-done | bytes 7340048
  (256 shorter events, 235.6 us)
Async XLA Ops:
  7.2 129.0 %all-gather.2.cloned.1.call-start = ((), (), s32[]{:S(2)}) async-start(), calls=%async_computation | async-start | bytes 3727360 | tf_op jit(solution)/shard_map/all_gather | solution.py:159
  25.4 547.3 %all-reduce.3.cloned.1.call-start = ((), (), s32[]{:S(2)}) async-start(), calls=%async_computation.1 | async-start | bytes 14680064
  32.0 10.5 %copy-start.20 = (f32[3,16]{1,0:T(4,128)S(1)}, f32[3,16]{1,0:T(4,128)}, u32[]{:S(2)}) copy-start(f32[3,16]{1,0:T(4,128)} %param.17) | copy-start | bytes 580
  35.4 49.6 %collective-permute-start = (bf16[2,256,2048]{1,2,0:T(8,128)(2,1)}, bf16[2,256,2048]{1,2,0:T(8,128)(2,1)}, u32[]{:S(2)}, u32[]{:S(2)}) collective-permute-start(bf16[2,256,2048]{1,2,0:T(8,128)(2,1)} %get-tuple-element.189), channel_id=1, source_target_pairs={{0,2},{2,4},{4,6},{6,8},{8,10},{10,12},{12,14},{14,16},{16,18},{18... | collective-permute-start | bytes 6291464 | tf_op jit(solution)/shard_map/ppermute | solution.py:24
  41.2 48.9 %collective-permute-start.1 = (bf16[2,256,2048]{1,2,0:T(8,128)(2,1)}, bf16[2,256,2048]{1,2,0:T(8,128)(2,1)}, u32[]{:S(2)}, u32[]{:S(2)}) collective-permute-start(bf16[2,256,2048]{1,2,0:T(8,128)(2,1)} %get-tuple-element.190), channel_id=1, source_target_pairs={{2,0},{4,2},{6,4},{8,6},{10,8},{12,10},{14,12},{16,14},{18,16},{20... | collective-permute-start | bytes 6291464 | tf_op jit(solution)/shard_map/ppermute | solution.py:26
  42.9 7.9 %copy-start.13 = (s32[1,64,12]{1,0,2:T(1,128)S(1)}, s32[1,64,12]{1,0,2:T(1,128)}, u32[]{:S(2)}) copy-start(s32[1,64,12]{1,0,2:T(1,128)} %param.16) | copy-start | bytes 9220
  51.1 42.8 %copy-start.16 = (s32[4]{0:T(128)}, s32[4]{0:T(128)S(1)}, u32[]{:S(2)}) copy-start(s32[4]{0:T(128)S(1)} %get-tuple-element.150) | copy-start | bytes 52
  51.1 42.8 %copy-start.18 = (s32[4]{0:T(128)}, s32[4]{0:T(128)S(1)}, u32[]{:S(2)}) copy-start(s32[4]{0:T(128)S(1)} %get-tuple-element.152) | copy-start | bytes 52
  163.3 6.7 %copy-start.6 = (bf16[4,512,4,128]{1,3,2,0:T(8,128)(2,1)S(1)}, bf16[4,512,4,128]{1,3,2,0:T(8,128)(2,1)}, u32[]{:S(2)}) copy-start(bf16[4,512,4,128]{1,3,2,0:T(8,128)(2,1)} %custom-call.8) | copy-start | bytes 6291460
  188.6 12.0 %slice-start = ((s8[4325376]{0:T(1024)(128)(4,1)}), s8[4194304]{0:T(1024)(128)(4,1)S(1)}, s32[]{:S(2)}) async-start(s8[4325376]{0:T(1024)(128)(4,1)} %bitcast.213), calls=%async_computation.2 | async-start | bytes 8388608 | tf_op jit(solution)/shard_map/while
  188.8 11.9 %slice-start.1 = ((s8[4325376]{0:T(1024)(128)(4,1)}), s8[131072]{0:T(1024)(128)(4,1)S(1)}, s32[]{:S(2)}) async-start(s8[4325376]{0:T(1024)(128)(4,1)} %bitcast.213), calls=%async_computation.3 | async-start | bytes 262144 | tf_op jit(solution)/shard_map/while
  223.4 12.0 %slice-start = ((s8[4325376]{0:T(1024)(128)(4,1)}), s8[4194304]{0:T(1024)(128)(4,1)S(1)}, s32[]{:S(2)}) async-start(s8[4325376]{0:T(1024)(128)(4,1)} %bitcast.213), calls=%async_computation.2 | async-start | bytes 8388608 | tf_op jit(solution)/shard_map/while
  223.5 11.9 %slice-start.1 = ((s8[4325376]{0:T(1024)(128)(4,1)}), s8[131072]{0:T(1024)(128)(4,1)S(1)}, s32[]{:S(2)}) async-start(s8[4325376]{0:T(1024)(128)(4,1)} %bitcast.213), calls=%async_computation.3 | async-start | bytes 262144 | tf_op jit(solution)/shard_map/while
  258.1 12.0 %slice-start = ((s8[4325376]{0:T(1024)(128)(4,1)}), s8[4194304]{0:T(1024)(128)(4,1)S(1)}, s32[]{:S(2)}) async-start(s8[4325376]{0:T(1024)(128)(4,1)} %bitcast.213), calls=%async_computation.2 | async-start | bytes 8388608 | tf_op jit(solution)/shard_map/while
  258.2 11.9 %slice-start.1 = ((s8[4325376]{0:T(1024)(128)(4,1)}), s8[131072]{0:T(1024)(128)(4,1)S(1)}, s32[]{:S(2)}) async-start(s8[4325376]{0:T(1024)(128)(4,1)} %bitcast.213), calls=%async_computation.3 | async-start | bytes 262144 | tf_op jit(solution)/shard_map/while
  292.8 12.1 %slice-start = ((s8[4325376]{0:T(1024)(128)(4,1)}), s8[4194304]{0:T(1024)(128)(4,1)S(1)}, s32[]{:S(2)}) async-start(s8[4325376]{0:T(1024)(128)(4,1)} %bitcast.213), calls=%async_computation.2 | async-start | bytes 8388608 | tf_op jit(solution)/shard_map/while
  292.9 11.9 %slice-start.1 = ((s8[4325376]{0:T(1024)(128)(4,1)}), s8[131072]{0:T(1024)(128)(4,1)S(1)}, s32[]{:S(2)}) async-start(s8[4325376]{0:T(1024)(128)(4,1)} %bitcast.213), calls=%async_computation.3 | async-start | bytes 262144 | tf_op jit(solution)/shard_map/while
  309.1 10.8 %copy-start.9 = (bf16[4,512,4,128]{1,3,2,0:T(8,128)(2,1)}, bf16[4,512,4,128]{1,3,2,0:T(8,128)(2,1)S(1)}, u32[]{:S(2)}) copy-start(bf16[4,512,4,128]{1,3,2,0:T(8,128)(2,1)S(1)} %get-tuple-element.90) | copy-start | bytes 6291460
  346.4 9.0 %copy-start.5 = (f32[256,4,4,128]{3,0,2,1:T(8,128)S(1)}, f32[256,4,4,128]{3,0,2,1:T(8,128)}, u32[]{:S(2)}) copy-start(f32[256,4,4,128]{3,0,2,1:T(8,128)} %get-tuple-element.181) | copy-start | bytes 6291460
  351.4 180.5 %collective-permute-start.2 = (f32[2,256,2048]{2,1,0:T(8,128)}, f32[2,256,2048]{2,1,0:T(8,128)}, u32[]{:S(2)}, u32[]{:S(2)}) collective-permute-start(f32[2,256,2048]{2,1,0:T(8,128)} %pad_maximum_fusion.2), channel_id=1, source_target_pairs={{0,2},{2,4},{4,6},{6,8},{8,10},{10,12},{12,14},{14,16},{16,18},{18... | collective-permute-start | bytes 12582920 | tf_op jit(solution)/shard_map/ppermute | solution.py:36
  363.5 6.1 %copy-start.21 = (u32[128]{0:T(128)S(1)}, u32[128]{0:T(128)}, u32[]{:S(2)}) copy-start(u32[128]{0:T(128)} %constant.151) | copy-start | bytes 1540
  368.3 170.2 %collective-permute-start.3 = (f32[2,256,2048]{2,1,0:T(8,128)}, f32[2,256,2048]{2,1,0:T(8,128)}, u32[]{:S(2)}, u32[]{:S(2)}) collective-permute-start(f32[2,256,2048]{2,1,0:T(8,128)} %pad_maximum_fusion.3), channel_id=1, source_target_pairs={{2,0},{4,2},{6,4},{8,6},{10,8},{12,10},{14,12},{16,14},{18,16},{20... | collective-permute-start | bytes 12582920 | tf_op jit(solution)/shard_map/ppermute | solution.py:36
  398.5 5.6 copy-start.10
  524.7 5.0 copy-start.4
  (27 other events, 90.0 us)
Sparse Core Ops, SparseCore 0:
  25.5 110.6 all-gather.1
  331.6 240.9 all-reduce.2
where the time goes:
time: 601 us; the launch traced here: 591 us
  local copies, waits for them, and re-layouts  144 us (24%)
  blocking collectives  113 us (19%)
  matrix products  110 us (18%)
  waiting for transfers between devices  104 us (17%)
  other arithmetic  91.3 us (15%)
  between operations  14.9 us (2%)
  starting transfers between devices  12.4 us (2%)
    psum x1, blocking collectives, shards(): bias_total = lax.psum(jnp.stack(level_parts), ('seq', 'batch'))  113 us
    all_gather x1, waiting for transfers between devices, shards(): summary_table = lax.all_gather(own_summary[None], 'seq', axis=0, tiled=True)  38.4 us
    ppermute x1, waiting for transfers between devices, with_halo(): lax.ppermute(tail, axis, [(i, (i + 1) % count) for i in range(ends)])  33.3 us
    sub x4, matrix products, attend_group(): raised = jnp.exp(scores - row_max)  30.4 us
    unnamed x3, waiting for transfers between devices  27.7 us
    dot_general x4, matrix products, attend_group(): jnp.einsum('qge,kge->gqk', out_grad, all_values, preferred_element_type=j...  23.3 us
    unnamed x41, local copies, waits for them, and re-layouts  20.6 us
    convert_element_type x4, other arithmetic, attend_group(): weights_low = weights.astype(jnp.bfloat16)  18.7 us
  transfers between devices with their start and end apart: 6, of which 4 were waited for; matrix products, arithmetic and copies ran while one was open for 20% of the time, Pallas kernels for 0%

commit v1 on v0

v1 whole, which is shorter than its diff:
```python
import functools
import math

import jax
import jax.numpy as jnp
from jax import lax
from jax.experimental import pallas as pl
from jax.experimental.pallas import tpu as pltpu
from jax.sharding import PartitionSpec as P

HEADS = 16
DIM = 128
WIDTH = HEADS * DIM
LEAF = 512
RIM = 256
BLOCKS = 64
PAIRS = 8
PAIR = 2 * DIM
NEAR = LEAF + 2 * RIM
FAR = 32
LIST = NEAR + FAR
SCALE = 1.0 / math.sqrt(DIM)
LOG2E = math.log2(math.e)
BIG = 1e30
MESH = pl.DeviceIdType.MESH
F32 = jnp.float32
BF16 = jnp.bfloat16
HALF = WIDTH // 2

NT = (((1,), (1,)), ((), ()))
TN = (((0,), (0,)), ((), ()))
NN = (((1,), (0,)), ((), ()))

CHUNKS = ((0, 256), (256, 256), (512, 256), (768, 256), (1024, FAR))


def dot(a, b, dims=NN):
    return lax.dot_general(a, b, dims, preferred_element_type=F32)


def selector(lists_ref, me):
    row = lax.broadcasted_iota(jnp.int32, (FAR, 4 * BLOCKS), 0)
    col = lax.broadcasted_iota(jnp.int32, (FAR, 4 * BLOCKS), 1)
    block = jnp.full((FAR, 4 * BLOCKS), -1, jnp.int32)
    first = 0
    for level, count in enumerate((4, 2, 1)):
        for slot in range(4):
            listed = lists_ref[me, level * 4 + slot]
            block = jnp.where((row >= first) & (row < first + count), listed, block)
            first += count
    one = (row < 16) & (col == block * 4 + (row & 3))
    two = (row >= 16) & (row < 24) & ((col >> 1) == block * 2 + (row & 1))
    three = (row >= 24) & (row < 28) & ((col >> 2) == block)
    return jnp.where(one, 1.0, 0.0) + jnp.where(two, 0.5, 0.0) + jnp.where(three, 0.25, 0.0)


def kernel(
    q_hbm, k_hbm, v_hbm, g_hbm, lists_ref, bias_ref,
    o_hbm, dq_hbm, dk_hbm, dv_hbm, level_ref,
    kx, vx, qx, gx, ox, dqx, own, to_down, to_up, from_up, from_down,
    table, gtable, zbuf, col32, r1b, r2s, r2b, r3s, r3b, far_grad,
    sel_ref, lvl, lvz, lvx, lvy, lvc, s_ref, w_ref, d_ref,
    fwd_send, fwd_recv, bwd_send, bwd_recv, in_sem, out_sem,
    z_send, z_recv, a1_send, a1_recv, a2_send, a2_recv,
    r1_send, r1_recv, r2_send, r2_recv, r3_send, r3_recv,
    l_send, l_recv, c_send, c_recv,
):
    me = lax.axis_index("seq")
    core = lax.axis_index("batch")
    z = lax.rem(me, 4)
    x = lax.rem(lax.div(me, 4), 4)
    y = lax.div(me, 16)
    up = lax.rem(me + 1, BLOCKS)
    down = lax.rem(me + BLOCKS - 1, BLOCKS)

    def ahead(c, d):
        return lax.rem(c + d, 4)

    def behind(c, d):
        return lax.rem(c + 4 - d, 4)

    def at_y(c):
        return c * 16 + x * 4 + z

    def at_x(c):
        return y * 16 + c * 4 + z

    def at_z(c):
        return y * 16 + x * 4 + c

    def remote(src, dst, send, recv, to):
        return pltpu.make_async_remote_copy(
            src_ref=src, dst_ref=dst, send_sem=send, recv_sem=recv,
            device_id={"seq": to}, device_id_type=MESH,
        )

    barrier = pltpu.get_barrier_semaphore()
    partners = [up, down]
    for d in (1, 2, 3):
        partners += [at_z(ahead(z, d)), at_x(ahead(x, d)), at_y(ahead(y, d))]
    for to in partners:
        pl.semaphore_signal(barrier, inc=1, device_id={"seq": to}, device_id_type=MESH)
    pl.semaphore_signal(barrier, inc=1, device_id={"batch": 1 - core}, device_id_type=MESH)

    def cols(p):
        return pl.ds(pl.multiple_of(p * PAIR, PAIR), PAIR)

    def load(p):
        return [
            pltpu.make_async_copy(k_hbm.at[:, cols(p)], kx.at[p, pl.ds(RIM, LEAF), :], in_sem.at[p, 0]),
            pltpu.make_async_copy(v_hbm.at[:, cols(p)], vx.at[p, pl.ds(RIM, LEAF), :], in_sem.at[p, 1]),
            pltpu.make_async_copy(q_hbm.at[:, cols(p)], qx.at[p], in_sem.at[p, 2]),
            pltpu.make_async_copy(g_hbm.at[:, cols(p)], gx.at[p], in_sem.at[p, 3]),
        ]

    def rims(p):
        lower, upper = pl.ds(0, RIM), pl.ds(RIM, RIM)
        low_rim, high_rim = pl.ds(0, RIM), pl.ds(RIM + LEAF, RIM)
        found = []
        for i, (src, dst) in enumerate(((k_hbm, kx), (v_hbm, vx))):
            found.append(remote(src.at[upper, cols(p)], dst.at[p, low_rim, :], fwd_send.at[p, i, 0], fwd_recv.at[p, i, 0], up))
            found.append(remote(src.at[lower, cols(p)], dst.at[p, high_rim, :], fwd_send.at[p, i, 1], fwd_recv.at[p, i, 1], down))
        return found

    def back(p):
        return [
            remote(to_up.at[p], from_down.at[p], bwd_send.at[p, 0], bwd_recv.at[p, 0], up),
            remote(to_down.at[p], from_up.at[p], bwd_send.at[p, 1], bwd_recv.at[p, 1], down),
        ]

    @pl.loop(0, PAIRS)
    def _(p):
        for c in load(p)[:2]:
            c.start()

    @pl.loop(0, PAIRS)
    def _(p):
        for c in load(p)[2:]:
            c.start()

    pl.semaphore_wait(barrier, 12)
    for c in rims(0):
        c.start()

    sel_ref[...] = selector(lists_ref, me).astype(BF16)

    pool_row = lax.broadcasted_iota(jnp.int32, (8, LEAF), 0)
    pool_tok = lax.broadcasted_iota(jnp.int32, (8, LEAF), 1) // 128
    pool_k = jnp.where(pool_tok == pool_row, 1.0 / 128, 0.0).astype(BF16)
    pool_v = jnp.where(pool_tok + 4 == pool_row, 1.0 / 128, 0.0).astype(BF16)

    @pl.loop(0, PAIRS)
    def _(p):
        for c in load(p)[:2]:
            c.wait()
        mine = pl.ds(RIM, LEAF)
        zbuf[z, :, cols(p)] = dot(pool_k, kx[p, mine, :]) + dot(pool_v, vx[p, mine, :])

    def gather_z(d):
        return remote(zbuf.at[z], zbuf.at[z], z_send.at[d - 1], z_recv.at[d - 1], at_z(ahead(z, d)))

    for d in (1, 2, 3):
        gather_z(d).start()
    @pl.loop(1, PAIRS)
    def _(p):
        for c in rims(p):
            c.start()

    for d in (1, 2, 3):
        gather_z(d).wait_recv()
    for i in (0, 1):
        for c in range(4):
            col32[4 * c : 4 * c + 4, :] = zbuf[c, 4 * i : 4 * i + 4, :]
        table[i, y, x] = col32[...].astype(BF16)

    def gather_one(d):
        return [
            remote(table.at[0, y, x], table.at[0, y, x], a1_send.at[0, d - 1], a1_recv.at[0, d - 1], at_x(ahead(x, d))),
            remote(table.at[1, y, x], table.at[1, y, x], a1_send.at[1, d - 1], a1_recv.at[1, d - 1], at_y(ahead(y, d))),
        ]

    def gather_two(d):
        return [
            remote(table.at[0, y], table.at[0, y], a2_send.at[0, d - 1], a2_recv.at[0, d - 1], at_y(ahead(y, d))),
            remote(table.at[1, :, x], table.at[1, :, x], a2_send.at[1, d - 1], a2_recv.at[1, d - 1], at_x(ahead(x, d))),
        ]

    for d in (1, 2, 3):
        for c in gather_one(d):
            c.start()
    for d in (1, 2, 3):
        for c in gather_one(d):
            c.wait_recv()
    for d in (1, 2, 3):
        for c in gather_two(d):
            c.start()
    for d in (1, 2, 3):
        for c in gather_two(d):
            c.wait_recv()

    lane_sel = lax.broadcasted_iota(jnp.int32, (FAR, 128), 1)
    far_row = lax.broadcasted_iota(jnp.int32, (FAR, 1), 0)
    lvl[...] = jnp.zeros_like(lvl)
    low_gap = jnp.where(me == 0, BIG, 0.0).astype(F32)
    high_gap = jnp.where(me == BLOCKS - 1, BIG, 0.0).astype(F32)
    gaps = (low_gap, None, None, high_gap, None)
    factor = SCALE * LOG2E

    def head(p, h):
        lanes = slice(h * DIM, h * DIM + DIM)
        head_no = 2 * p + h
        bias = jnp.where(
            far_row < 16, bias_ref[0, head_no] + math.log(128),
            jnp.where(far_row < 24, bias_ref[1, head_no] + math.log(256),
                      jnp.where(far_row < 28, bias_ref[2, head_no] + math.log(512), -BIG)))
        bias = bias * LOG2E
        query = qx[p, :, lanes]
        grad = gx[p, :, lanes]
        top = None
        for (first, rows), gap in zip(CHUNKS, gaps):
            s = dot(kx[p, first : first + rows, lanes], query, NT) * factor
            if rows == FAR:
                s = s + bias
            s_ref[h, first : first + rows, :] = s
            peak = jnp.max(s, axis=0, keepdims=True)
            if gap is not None:
                peak = peak - gap
            top = peak if top is None else jnp.maximum(top, peak)
        total = jnp.zeros((1, LEAF), F32)
        for (first, rows), gap in zip(CHUNKS, gaps):
            base = top if gap is None else top + gap
            e = jnp.exp2(s_ref[h, first : first + rows, :] - base)
            s_ref[h, first : first + rows, :] = e
            total = total + jnp.sum(e, axis=0, keepdims=True)
        inverse = 1.0 / total
        for first, rows in CHUNKS:
            w_ref[h, first : first + rows, :] = (s_ref[h, first : first + rows, :] * inverse).astype(BF16)
        out = dot(vx[p, :, lanes], w_ref[h], TN).T.astype(BF16)
        ox[p, :, lanes] = out
        ones = jnp.ones((8, DIM), F32)
        row_dot = lax.dot_general(
            ones, out.astype(F32) * grad.astype(F32), NT,
            precision=lax.Precision.HIGHEST, preferred_element_type=F32)[0:1, :]
        for first, rows in CHUNKS:
            dw = dot(vx[p, first : first + rows, lanes], grad, NT)
            ds = s_ref[h, first : first + rows, :] * inverse * (dw - row_dot)
            d_ref[h, first : first + rows, :] = ds.astype(BF16)
            if rows == FAR:
                sums = jnp.sum(ds, axis=1, keepdims=True)
                lvl[...] += jnp.where(lane_sel == head_no, sums, 0.0)
        dqx[p, :, lanes] = (dot(kx[p, :, lanes], d_ref[h], TN) * SCALE).T.astype(BF16)
        dk = dot(d_ref[h], query) * SCALE
        dv = dot(w_ref[h], grad)
        for i, term in enumerate((dk, dv)):
            to_down[p, i, :, lanes] = term[:RIM].astype(BF16)
            own[p, i, :, lanes] = term[RIM : RIM + LEAF]
            to_up[p, i, :, lanes] = term[RIM + LEAF : NEAR].astype(BF16)
        return dk[NEAR:], dv[NEAR:]

    def half_lanes(half):
        return pl.ds(half * HALF, HALF)

    def r1(half, d):
        n = half_lanes(half)
        yp, xp = ahead(y, d), ahead(x, d)
        return [
            remote(gtable.at[0, yp, :, :, n], r1b.at[0, y, :, :, n], r1_send.at[half, 0, d - 1], r1_recv.at[half, 0, d - 1], at_y(yp)),
            remote(gtable.at[1, :, xp, :, n], r1b.at[1, x, :, :, n], r1_send.at[half, 1, d - 1], r1_recv.at[half, 1, d - 1], at_x(xp)),
        ]

    def r2(half, d):
        n = half_lanes(half)
        yp, xp = ahead(y, d), ahead(x, d)
        return [
            remote(r2s.at[0, xp, :, n], r2b.at[0, x, :, n], r2_send.at[half, 0, d - 1], r2_recv.at[half, 0, d - 1], at_x(xp)),
            remote(r2s.at[1, yp, :, n], r2b.at[1, y, :, n], r2_send.at[half, 1, d - 1], r2_recv.at[half, 1, d - 1], at_y(yp)),
        ]

    def r3(half, d):
        n = half_lanes(half)
        zp = ahead(z, d)
        return [remote(r3s.at[zp, :, n], r3b.at[z, :, n], r3_send.at[half, d - 1], r3_recv.at[half, d - 1], at_z(zp))]

    def go(step, half):
        for d in (1, 2, 3):
            for c in step(half, d):
                c.start()

    def got(step, half):
        for d in (1, 2, 3):
            for c in step(half, d):
                c.wait_recv()

    def r1_finish(half):
        n = half_lanes(half)
        got(r1, half)
        for i in range(4):
            sum_k = gtable[0, y, i, :, n].astype(F32)
            sum_v = gtable[1, i, x, :, n].astype(F32)
            for d in (1, 2, 3):
                sum_k = sum_k + r1b[0, behind(y, d), i, :, n].astype(F32)
                sum_v = sum_v + r1b[1, behind(x, d), i, :, n].astype(F32)
            r2s[0, i, :, n] = sum_k.astype(BF16)
            r2s[1, i, :, n] = sum_v.astype(BF16)
        go(r2, half)

    def r2_finish(half):
        n = half_lanes(half)
        got(r2, half)
        for j, c in enumerate((x, y)):
            total = r2s[j, c, :, n].astype(F32)
            for d in (1, 2, 3):
                total = total + r2b[j, behind(c, d), :, n].astype(F32)
            col32[:, n] = total
            for i in range(4):
                r3s[i, 4 * j : 4 * j + 4, n] = col32[4 * i : 4 * i + 4, n]
        go(r3, half)

    def r3_finish(half):
        n = half_lanes(half)
        got(r3, half)
        total = r3s[z, :, n]
        for d in (1, 2, 3):
            total = total + r3b[behind(z, d), :, n]
        far_grad[:, n] = total * (1.0 / 128)

    def outs(p):
        return [
            pltpu.make_async_copy(ox.at[p], o_hbm.at[:, cols(p)], out_sem.at[p, 0]),
            pltpu.make_async_copy(dqx.at[p], dq_hbm.at[:, cols(p)], out_sem.at[p, 1]),
            pltpu.make_async_copy(qx.at[p], dk_hbm.at[:, cols(p)], out_sem.at[p, 2]),
            pltpu.make_async_copy(gx.at[p], dv_hbm.at[:, cols(p)], out_sem.at[p, 3]),
        ]

    @pl.loop(0, PAIRS)
    def _(p):
        sel = sel_ref[...]
        for i, dst in enumerate((kx, vx)):
            rows = table[i, :, :, :, cols(p)].reshape(4 * BLOCKS, PAIR)
            dst[p, NEAR:LIST, :] = dot(sel, rows).astype(BF16)
        for c in load(p)[2:]:
            c.wait()
        for c in rims(p):
            c.wait_recv()
        first = head(p, 0)
        second = head(p, 1)
        for c in back(p):
            c.start()
        for c in outs(p)[:2]:
            c.start()
        for i in (0, 1):
            rows = jnp.concatenate([first[i], second[i]], axis=1).astype(BF16)
            gtable[i, :, :, :, cols(p)] = dot(sel, rows, TN).astype(BF16).reshape(4, 4, 16, PAIR)

        @pl.when(p == 3)
        def _():
            go(r1, 0)

        @pl.when(p == 4)
        def _():
            r1_finish(0)

        @pl.when(p == 5)
        def _():
            r2_finish(0)

    go(r1, 1)

    level_no = lax.broadcasted_iota(jnp.int32, (8, FAR), 0)
    list_row = lax.broadcasted_iota(jnp.int32, (8, FAR), 1)
    level_of = jnp.where(list_row < 16, 0, jnp.where(list_row < 24, 1, jnp.where(list_row < 28, 2, 9)))
    pick = jnp.where(level_no == level_of, 1.0, 0.0).astype(F32)
    lvy[y] = lax.dot_general(pick, lvl[...], NN, precision=lax.Precision.HIGHEST, preferred_element_type=F32)

    def level_copy(buf, c, step, d, to):
        return remote(buf.at[c], buf.at[c], l_send.at[step, d - 1], l_recv.at[step, d - 1], to)

    def level_steps(step):
        buf, c, at = ((lvy, y, at_y), (lvx, x, at_x), (lvz, z, at_z))[step]
        return [level_copy(buf, c, step, d, at(ahead(c, d))) for d in (1, 2, 3)]

    def level_sum(step):
        for c in level_steps(step):
            c.wait_recv()
        buf = (lvy, lvx, lvz)[step]
        return (buf[0] + buf[1]) + (buf[2] + buf[3])

    for c in level_steps(0):
        c.start()

    def settle(p):
        for c in back(p):
            c.wait_recv()
        for i, dst in enumerate((qx, gx)):
            for r in range(4):
                tokens = pl.ds(128 * r, 128)
                total = own[p, i, tokens, :] + far_grad[4 * i + r : 4 * i + r + 1, cols(p)]
                if r < 2:
                    total = total + from_down[p, i, tokens, :].astype(F32)
                else:
                    total = total + from_up[p, i, pl.ds(128 * (r - 2), 128), :].astype(F32)
                dst[p, tokens, :] = total.astype(BF16)
        for c in outs(p)[2:]:
            c.start()

    r3_finish(0)

    @pl.loop(0, 4)
    def _(p):
        settle(p)

    lvx[x] = level_sum(0)
    for c in level_steps(1):
        c.start()
    r1_finish(1)
    lvz[z] = level_sum(1)
    for c in level_steps(2):
        c.start()
    r2_finish(1)
    lvc[core] = level_sum(2)
    swap = pltpu.make_async_remote_copy(
        src_ref=lvc.at[core], dst_ref=lvc.at[core], send_sem=c_send, recv_sem=c_recv,
        device_id={"batch": 1 - core}, device_id_type=MESH)
    swap.start()
    r3_finish(1)

    @pl.loop(4, PAIRS)
    def _(p):
        settle(p)

    swap.wait_recv()
    level_ref[...] = ((lvc[0] + lvc[1]) * (1.0 / math.sqrt(2 * BLOCKS * LEAF)))[0:3, 0:HEADS]

    swap.wait_send()
    for step in range(3):
        for c in level_steps(step):
            c.wait_send()
    for d in (1, 2, 3):
        gather_z(d).wait_send()
        for c in gather_one(d) + gather_two(d):
            c.wait_send()
        for half in (0, 1):
            for c in r1(half, d) + r2(half, d) + r3(half, d):
                c.wait_send()

    @pl.loop(0, PAIRS)
    def _(p):
        for c in rims(p) + back(p):
            c.wait_send()
        for c in outs(p):
            c.wait()


def shards(queries, key_vectors, values, out_grad, far_lists, level_bias):
    any_spec = pl.BlockSpec(memory_space=pl.ANY)
    smem = pl.BlockSpec(memory_space=pltpu.SMEM)
    dma = pltpu.SemaphoreType.DMA
    outs = pl.pallas_call(
        kernel,
        out_shape=[jax.ShapeDtypeStruct((LEAF, WIDTH), BF16)] * 4 + [jax.ShapeDtypeStruct((3, HEADS), F32)],
        in_specs=[any_spec] * 4 + [smem] * 2,
        out_specs=[any_spec] * 4 + [pl.BlockSpec(memory_space=pltpu.VMEM)],
        scratch_shapes=[
            pltpu.VMEM((PAIRS, LIST, PAIR), BF16),
            pltpu.VMEM((PAIRS, LIST, PAIR), BF16),
            pltpu.VMEM((PAIRS, LEAF, PAIR), BF16),
            pltpu.VMEM((PAIRS, LEAF, PAIR), BF16),
            pltpu.VMEM((PAIRS, LEAF, PAIR), BF16),
            pltpu.VMEM((PAIRS, LEAF, PAIR), BF16),
            pltpu.VMEM((PAIRS, 2, LEAF, PAIR), F32),
            pltpu.VMEM((PAIRS, 2, RIM, PAIR), BF16),
            pltpu.VMEM((PAIRS, 2, RIM, PAIR), BF16),
            pltpu.VMEM((PAIRS, 2, RIM, PAIR), BF16),
            pltpu.VMEM((PAIRS, 2, RIM, PAIR), BF16),
            pltpu.VMEM((2, 4, 4, 16, WIDTH), BF16),
            pltpu.VMEM((2, 4, 4, 16, WIDTH), BF16),
            pltpu.VMEM((4, 8, WIDTH), F32),
            pltpu.VMEM((16, WIDTH), F32),
            pltpu.VMEM((2, 4, 4, 16, WIDTH), BF16),
            pltpu.VMEM((2, 4, 16, WIDTH), BF16),
            pltpu.VMEM((2, 4, 16, WIDTH), BF16),
            pltpu.VMEM((4, 8, WIDTH), F32),
            pltpu.VMEM((4, 8, WIDTH), F32),
            pltpu.VMEM((8, WIDTH), F32),
            pltpu.VMEM((FAR, 4 * BLOCKS), BF16),
            pltpu.VMEM((FAR, 128), F32),
            pltpu.VMEM((4, 8, 128), F32),
            pltpu.VMEM((4, 8, 128), F32),
            pltpu.VMEM((4, 8, 128), F32),
            pltpu.VMEM((2, 8, 128), F32),
            pltpu.VMEM((2, LIST, LEAF), F32),
            pltpu.VMEM((2, LIST, LEAF), BF16),
            pltpu.VMEM((2, LIST, LEAF), BF16),
            dma((PAIRS, 2, 2)), dma((PAIRS, 2, 2)), dma((PAIRS, 2)), dma((PAIRS, 2)),
            dma((PAIRS, 4)), dma((PAIRS, 4)),
            dma((3,)), dma((3,)), dma((2, 3)), dma((2, 3)), dma((2, 3)), dma((2, 3)),
            dma((2, 2, 3)), dma((2, 2, 3)), dma((2, 2, 3)), dma((2, 2, 3)), dma((2, 3)), dma((2, 3)),
            dma((3, 3)), dma((3, 3)), dma, dma,
        ],
        compiler_params=pltpu.CompilerParams(
            collective_id=0, has_side_effects=True, vmem_limit_bytes=62 * 1024 * 1024),
        cost_estimate=pl.CostEstimate(
            flops=12 * HEADS * LEAF * LIST * DIM, bytes_accessed=8 * LEAF * WIDTH * 2,
            transcendentals=HEADS * LEAF * LIST),
    )(queries[0], key_vectors[0], values[0], out_grad[0], far_lists[0], level_bias)
    return tuple(o[None] for o in outs[:4]) + (outs[4],)


def solution(mesh):
    token = P("batch", "seq", None)
    return jax.shard_map(
        shards,
        mesh=mesh,
        in_specs=(token, token, token, token, P("batch", None, None), P()),
        out_specs=(token, token, token, token, P()),
        check_vma=False,
    )
```

time: 601 us -> 178 us (0.30); the launches traced: 591 us -> 178 us
  Pallas kernels: 0 us -> 166 us
  local copies, waits for them, and re-layouts: 144 us -> 11.3 us
  blocking collectives: 113 us -> 0 us
  matrix products: 110 us -> 0 us
  waiting for transfers between devices: 104 us -> 0 us
  other arithmetic: 91.3 us -> 0 us
  between operations: 14.9 us -> 0.65 us
  starting transfers between devices: 12.4 us -> 0 us
    pallas_call x0 -> x1, Pallas kernels: none -> 166 us  [shards(): pl.pallas_call(kernel, out_shape=[jax.ShapeDtypeStruct((LEAF, WIDTH), BF1...]
    psum x1 -> x0, blocking collectives: 113 us -> none  [shards(): bias_total = lax.psum(jnp.stack(level_parts), ('seq', 'batch'))]
    dot_general x23 -> x0, matrix products: 79.7 us -> none  [the longest x4 23.3 us: attend_group(): jnp.einsum('qge,kge->gqk', out_grad, all_values, preferred_element_type=j...]
    slice x24 -> x0, local copies, waits for them, and re-layouts: 48.1 us -> none  [the longest x4 12.9 us: shards(): downward = jnp.stack([key_terms[:RIM], value_terms[:RIM]])]
    all_gather x1 -> x0, waiting for transfers between devices: 38.4 us -> none  [shards(): summary_table = lax.all_gather(own_summary[None], 'seq', axis=0, tiled=True)]
    ppermute x4 -> x0, waiting for transfers between devices: 38.4 us -> none  [the longest x1 33.3 us: with_halo(): lax.ppermute(tail, axis, [(i, (i + 1) % count) for i in range(ends)])]
    sub x4 -> x0, matrix products: 30.4 us -> none  [attend_group(): raised = jnp.exp(scores - row_max)]
    unnamed x3 -> x0, waiting for transfers between devices: 27.7 us -> none
  transfers between devices with their start and end apart: 6 -> 0, of which waited for: 4 -> 0; matrix products, arithmetic and copies ran while one was open for 20% -> 0% of each run, Pallas kernels for 0% -> 0%
where the time goes in v1:
time: 178 us
  Pallas kernels  166 us (93%)
  local copies, waits for them, and re-layouts  11.3 us (6%)
    pallas_call x1, Pallas kernels, shards(): pl.pallas_call(kernel, out_shape=[jax.ShapeDtypeStruct((LEAF, WIDTH), BF1...  166 us
    unnamed x14, local copies, waits for them, and re-layouts  11.3 us

profile of v1, /device:TPU:1, one launch (start us, length us, event | category | flops | bytes accessed | tf_op | source)
XLA Modules:
  0.0 178.2 jit_solution(9251970508440342473)
XLA Ops:
  0.6 1.4 copy.11
  2.0 166.2 %shard_map.101 = (bf16[512,2048]{1,0:T(8,128)(2,1)}, bf16[512,2048]{1,0:T(8,128)(2,1)}, bf16[512,2048]{1,0:T(8,128)(2,1)}, bf16[512,2048]{1,0:T(8,128)(2,1)}, f32[3,16]{1,0:T(4,128)}) custom-call(bf16[512,2048]{1,0:T(8,128)(2,1)} %bitcast.14, bf16[512,2048]{1,0:T(8,128)(2,1)} %bitcast.15, bf16[512,2048]{1,0:T(8,128)(2,1)} %bitcast.16, ...), custom_call_target="tpu_custom_call" | custom-call | flops 13287555072 | bytes 16777216 | tf_op jit(solution)/shard_map/pallas_call | solution.py:458
  168.2 0.0 copy-start.2
  168.2 3.3 %copy.17 = bf16[1,512,2048]{2,1,0:T(8,128)(2,1)} copy(bf16[1,512,2048]{2,1,0:T(8,128)(2,1)} %bitcast.12) | data formatting | bytes 4194304
  171.6 0.0 copy-done.2
  171.6 0.0 copy-start.1
  171.6 1.3 copy.18
  172.9 1.0 copy-done.1
  173.9 0.0 copy-start
  173.9 1.3 copy.19
  175.2 1.0 copy-done
  176.3 0.0 copy-start.3
  176.3 1.3 copy.20
  177.6 0.0 copy-done.3
  177.6 0.6 copy.21
Async XLA Ops:
  168.2 3.3 %copy-start.2 = (bf16[512,2048]{1,0:T(8,128)(2,1)S(1)}, bf16[512,2048]{1,0:T(8,128)(2,1)}, u32[]{:S(2)}) copy-start(bf16[512,2048]{1,0:T(8,128)(2,1)} %get-tuple-element.11) | copy-start | bytes 6291460
  171.6 2.3 %copy-start.1 = (bf16[512,2048]{1,0:T(8,128)(2,1)S(1)}, bf16[512,2048]{1,0:T(8,128)(2,1)}, u32[]{:S(2)}) copy-start(bf16[512,2048]{1,0:T(8,128)(2,1)} %get-tuple-element.12) | copy-start | bytes 6291460
  173.9 2.3 %copy-start = (bf16[512,2048]{1,0:T(8,128)(2,1)S(1)}, bf16[512,2048]{1,0:T(8,128)(2,1)}, u32[]{:S(2)}) copy-start(bf16[512,2048]{1,0:T(8,128)(2,1)} %get-tuple-element.13) | copy-start | bytes 6291460
  176.3 1.3 copy-start.3

commit v2 on v1

--- a/solution.py
+++ b/solution.py
@@ -38,28 +38,31 @@
     return lax.dot_general(a, b, dims, preferred_element_type=F32)
 
 
-def selector(lists_ref, me):
-    row = lax.broadcasted_iota(jnp.int32, (FAR, 4 * BLOCKS), 0)
-    col = lax.broadcasted_iota(jnp.int32, (FAR, 4 * BLOCKS), 1)
-    block = jnp.full((FAR, 4 * BLOCKS), -1, jnp.int32)
+def selector(lists_ref, reader, block):
+    shape = (FAR, 64)
+    row = lax.broadcasted_iota(jnp.int32, shape, 0)
+    col = lax.broadcasted_iota(jnp.int32, shape, 1)
+    wanted = jnp.full(shape, -1, jnp.int32)
     first = 0
     for level, count in enumerate((4, 2, 1)):
         for slot in range(4):
-            listed = lists_ref[me, level * 4 + slot]
-            block = jnp.where((row >= first) & (row < first + count), listed, block)
+            listed = lists_ref[reader, level * 4 + slot]
+            wanted = jnp.where((row >= first) & (row < first + count), listed, wanted)
             first += count
-    one = (row < 16) & (col == block * 4 + (row & 3))
-    two = (row >= 16) & (row < 24) & ((col >> 1) == block * 2 + (row & 1))
-    three = (row >= 24) & (row < 28) & ((col >> 2) == block)
-    return jnp.where(one, 1.0, 0.0) + jnp.where(two, 0.5, 0.0) + jnp.where(three, 0.25, 0.0)
+    part = col & 3
+    one = (row < 16) & (part == (row & 3))
+    two = (row >= 16) & (row < 24) & ((part >> 1) == (row & 1))
+    share = jnp.where(one, 1.0, 0.0) + jnp.where(two, 0.5, 0.0) + jnp.where(row >= 24, 0.25, 0.0)
+    return jnp.where(wanted == block, share, 0.0).astype(BF16)
 
 
 def kernel(
     q_hbm, k_hbm, v_hbm, g_hbm, lists_ref, bias_ref,
     o_hbm, dq_hbm, dk_hbm, dv_hbm, level_ref,
     kx, vx, qx, gx, ox, dqx, own, to_down, to_up, from_up, from_down,
-    table, gtable, zbuf, col32, r1b, r2s, r2b, r3s, r3b, far_grad,
+    table, chosen, listed, dlisted, zbuf, col32, r2s, r2b, r3s, r3b, far_grad,
     sel_ref, lvl, lvz, lvx, lvy, lvc, s_ref, w_ref, d_ref,
+    fwd_relay, bwd_relay, relay_send, relay_recv,
     fwd_send, fwd_recv, bwd_send, bwd_recv, in_sem, out_sem,
     z_send, z_recv, a1_send, a1_recv, a2_send, a2_recv,
     r1_send, r1_recv, r2_send, r2_recv, r3_send, r3_recv,
@@ -72,6 +75,8 @@
     y = lax.div(me, 16)
     up = lax.rem(me + 1, BLOCKS)
     down = lax.rem(me + BLOCKS - 1, BLOCKS)
+    next_z = lax.rem(me + 4, BLOCKS)
+    last_z = lax.rem(me + BLOCKS - 4, BLOCKS)
 
     def ahead(c, d):
         return lax.rem(c + d, 4)
@@ -95,7 +100,7 @@
         )
 
     barrier = pltpu.get_barrier_semaphore()
-    partners = [up, down]
+    partners = [up, down, next_z, last_z]
     for d in (1, 2, 3):
         partners += [at_z(ahead(z, d)), at_x(ahead(x, d)), at_y(ahead(y, d))]
     for to in partners:
@@ -113,9 +118,10 @@
             pltpu.make_async_copy(g_hbm.at[:, cols(p)], gx.at[p], in_sem.at[p, 3]),
         ]
 
+    low_rim, high_rim = pl.ds(0, RIM), pl.ds(RIM + LEAF, RIM)
+
     def rims(p):
         lower, upper = pl.ds(0, RIM), pl.ds(RIM, RIM)
-        low_rim, high_rim = pl.ds(0, RIM), pl.ds(RIM + LEAF, RIM)
         found = []
         for i, (src, dst) in enumerate(((k_hbm, kx), (v_hbm, vx))):
             found.append(remote(src.at[upper, cols(p)], dst.at[p, low_rim, :], fwd_send.at[p, i, 0], fwd_recv.at[p, i, 0], up))
@@ -123,10 +129,65 @@
         return found
 
     def back(p):
-        return [
-            remote(to_up.at[p], from_down.at[p], bwd_send.at[p, 0], bwd_recv.at[p, 0], up),
-            remote(to_down.at[p], from_up.at[p], bwd_send.at[p, 1], bwd_recv.at[p, 1], down),
-        ]
+        found = []
+        for i in (0, 1):
+            found.append(remote(to_up.at[p, i], from_down.at[p, i], bwd_send.at[p, i, 0], bwd_recv.at[p, i, 0], up))
+            found.append(remote(to_down.at[p, i], from_up.at[p, i], bwd_send.at[p, i, 1], bwd_recv.at[p, i, 1], down))
+        return found
+
+    def detour(p, backward):
+        if backward:
+            sources, held, send, recv = (to_up.at[p, 1], to_down.at[p, 1]), bwd_relay.at[p], bwd_send, relay_recv.at[p, 1]
+        else:
+            sources = (v_hbm.at[pl.ds(RIM, RIM), cols(p)], v_hbm.at[pl.ds(0, RIM), cols(p)])
+            held, send, recv = fwd_relay.at[p], fwd_send, relay_recv.at[p, 0]
+        return (remote(sources[0], held, send.at[p, 1, 0], recv, at_z(0)),
+                remote(sources[1], held, send.at[p, 1, 1], recv, at_z(3)))
+
+    def onward(p, backward):
+        if backward:
+            held, send = bwd_relay.at[p], relay_send.at[p, 1]
+            return (remote(held, from_down.at[p, 1], send, bwd_recv.at[p, 1, 0], next_z),
+                    remote(held, from_up.at[p, 1], send, bwd_recv.at[p, 1, 1], last_z))
+        held, send = fwd_relay.at[p], relay_send.at[p, 0]
+        return (remote(held, vx.at[p, low_rim, :], send, fwd_recv.at[p, 1, 0], next_z),
+                remote(held, vx.at[p, high_rim, :], send, fwd_recv.at[p, 1, 1], last_z))
+
+    def send_out(p, backward):
+        key_up, key_down, value_up, value_down = back(p) if backward else rims(p)
+        far_up, far_down = detour(p, backward)
+        key_up.start()
+        key_down.start()
+
+        @pl.when(z == 3)
+        def _():
+            far_up.start()
+
+        @pl.when(z != 3)
+        def _():
+            value_up.start()
+
+        @pl.when(z == 0)
+        def _():
+            far_down.start()
+
+        @pl.when(z != 0)
+        def _():
+            value_down.start()
+
+    def relay(p, backward):
+        came_up, came_down = detour(p, backward)
+        on_up, on_down = onward(p, backward)
+
+        @pl.when(z == 0)
+        def _():
+            came_up.wait_recv()
+            on_up.start()
+
+        @pl.when(z == 3)
+        def _():
+            came_down.wait_recv()
+            on_down.start()
 
     @pl.loop(0, PAIRS)
     def _(p):
@@ -138,11 +199,15 @@
         for c in load(p)[2:]:
             c.start()
 
-    pl.semaphore_wait(barrier, 12)
-    for c in rims(0):
-        c.start()
-
-    sel_ref[...] = selector(lists_ref, me).astype(BF16)
+    pl.semaphore_wait(barrier, 14)
+    send_out(0, False)
+
+    col_block = lax.broadcasted_iota(jnp.int32, (FAR, 64), 1) // 4
+    key_block = y * 16 + col_block
+    value_block = (col_block // 4) * 16 + x * 4 + (col_block & 3)
+    for i in range(4):
+        sel_ref[0, i * FAR : (i + 1) * FAR, :] = selector(lists_ref, at_y(i), key_block)
+        sel_ref[1, i * FAR : (i + 1) * FAR, :] = selector(lists_ref, at_x(i), value_block)
 
     pool_row = lax.broadcasted_iota(jnp.int32, (8, LEAF), 0)
     pool_tok = lax.broadcasted_iota(jnp.int32, (8, LEAF), 1) // 128
@@ -161,42 +226,53 @@
 
     for d in (1, 2, 3):
         gather_z(d).start()
-    @pl.loop(1, PAIRS)
-    def _(p):
-        for c in rims(p):
-            c.start()
-
     for d in (1, 2, 3):
         gather_z(d).wait_recv()
     for i in (0, 1):
         for c in range(4):
             col32[4 * c : 4 * c + 4, :] = zbuf[c, 4 * i : 4 * i + 4, :]
-        table[i, y, x] = col32[...].astype(BF16)
+        table[i, (x, y)[i]] = col32[...].astype(BF16)
 
     def gather_one(d):
         return [
-            remote(table.at[0, y, x], table.at[0, y, x], a1_send.at[0, d - 1], a1_recv.at[0, d - 1], at_x(ahead(x, d))),
-            remote(table.at[1, y, x], table.at[1, y, x], a1_send.at[1, d - 1], a1_recv.at[1, d - 1], at_y(ahead(y, d))),
+            remote(table.at[0, x], table.at[0, x], a1_send.at[0, d - 1], a1_recv.at[0, d - 1], at_x(ahead(x, d))),
+            remote(table.at[1, y], table.at[1, y], a1_send.at[1, d - 1], a1_recv.at[1, d - 1], at_y(ahead(y, d))),
         ]
 
     def gather_two(d):
+        yp, xp = ahead(y, d), ahead(x, d)
         return [
-            remote(table.at[0, y], table.at[0, y], a2_send.at[0, d - 1], a2_recv.at[0, d - 1], at_y(ahead(y, d))),
-            remote(table.at[1, :, x], table.at[1, :, x], a2_send.at[1, d - 1], a2_recv.at[1, d - 1], at_x(ahead(x, d))),
+            remote(chosen.at[0, yp], listed.at[0, y], a2_send.at[0, d - 1], a2_recv.at[0, d - 1], at_y(yp)),
+            remote(chosen.at[1, xp], listed.at[1, x], a2_send.at[1, d - 1], a2_recv.at[1, d - 1], at_x(xp)),
         ]
 
     for d in (1, 2, 3):
         for c in gather_one(d):
             c.start()
+    send_out(1, False)
     for d in (1, 2, 3):
         for c in gather_one(d):
             c.wait_recv()
+    for i in (0, 1):
+        for n in range(0, WIDTH, 512):
+            rows = table[i, :, :, n : n + 512].reshape(64, 512)
+            chosen[i, :, :, n : n + 512] = dot(sel_ref[i], rows).astype(BF16).reshape(4, FAR, 512)
     for d in (1, 2, 3):
         for c in gather_two(d):
             c.start()
+    listed[0, y] = chosen[0, y]
+    listed[1, x] = chosen[1, x]
+
+    @pl.loop(2, PAIRS)
+    def _(p):
+        send_out(p, False)
+
     for d in (1, 2, 3):
         for c in gather_two(d):
             c.wait_recv()
+
+    for p in range(3):
+        relay(p, False)
 
     lane_sel = lax.broadcasted_iota(jnp.int32, (FAR, 128), 1)
     far_row = lax.broadcasted_iota(jnp.int32, (FAR, 1), 0)
@@ -264,8 +340,8 @@
         n = half_lanes(half)
         yp, xp = ahead(y, d), ahead(x, d)
         return [
-            remote(gtable.at[0, yp, :, :, n], r1b.at[0, y, :, :, n], r1_send.at[half, 0, d - 1], r1_recv.at[half, 0, d - 1], at_y(yp)),
-            remote(gtable.at[1, :, xp, :, n], r1b.at[1, x, :, :, n], r1_send.at[half, 1, d - 1], r1_recv.at[half, 1, d - 1], at_x(xp)),
+            remote(dlisted.at[0, y, :, n], dlisted.at[0, y, :, n], r1_send.at[half, 0, d - 1], r1_recv.at[half, 0, d - 1], at_y(yp)),
+            remote(dlisted.at[1, x, :, n], dlisted.at[1, x, :, n], r1_send.at[half, 1, d - 1], r1_recv.at[half, 1, d - 1], at_x(xp)),
         ]
 
     def r2(half, d):
@@ -292,16 +368,12 @@
                 c.wait_recv()
 
     def r1_finish(half):
-        n = half_lanes(half)
         got(r1, half)
-        for i in range(4):
-            sum_k = gtable[0, y, i, :, n].astype(F32)
-            sum_v = gtable[1, i, x, :, n].astype(F32)
-            for d in (1, 2, 3):
-                sum_k = sum_k + r1b[0, behind(y, d), i, :, n].astype(F32)
-                sum_v = sum_v + r1b[1, behind(x, d), i, :, n].astype(F32)
-            r2s[0, i, :, n] = sum_k.astype(BF16)
-            r2s[1, i, :, n] = sum_v.astype(BF16)
+        for i in (0, 1):
+            for first in range(0, HALF, 512):
+                n = pl.ds(half * HALF + first, 512)
+                terms = dot(sel_ref[i], dlisted[i, :, :, n].reshape(4 * FAR, 512), TN)
+                r2s[i, :, :, n] = terms.astype(BF16).reshape(4, 16, 512)
         go(r2, half)
 
     def r2_finish(half):
@@ -334,37 +406,44 @@
 
     @pl.loop(0, PAIRS)
     def _(p):
-        sel = sel_ref[...]
         for i, dst in enumerate((kx, vx)):
-            rows = table[i, :, :, :, cols(p)].reshape(4 * BLOCKS, PAIR)
-            dst[p, NEAR:LIST, :] = dot(sel, rows).astype(BF16)
+            rows = listed[i, :, :, cols(p)].astype(F32)
+            dst[p, NEAR:LIST, :] = ((rows[0] + rows[1]) + (rows[2] + rows[3])).astype(BF16)
         for c in load(p)[2:]:
             c.wait()
         for c in rims(p):
             c.wait_recv()
         first = head(p, 0)
         second = head(p, 1)
-        for c in back(p):
-            c.start()
+        send_out(p, True)
         for c in outs(p)[:2]:
             c.start()
-        for i in (0, 1):
-            rows = jnp.concatenate([first[i], second[i]], axis=1).astype(BF16)
-            gtable[i, :, :, :, cols(p)] = dot(sel, rows, TN).astype(BF16).reshape(4, 4, 16, PAIR)
+        for i, slot in ((0, y), (1, x)):
+            dlisted[i, slot, :, cols(p)] = jnp.concatenate([first[i], second[i]], axis=1).astype(BF16)
+
+        @pl.when(p < PAIRS - 3)
+        def _():
+            relay(p + 3, False)
+
+        @pl.when(p >= 2)
+        def _():
+            relay(p - 2, True)
 
         @pl.when(p == 3)
         def _():
             go(r1, 0)
 
-        @pl.when(p == 4)
+        @pl.when(p == 6)
         def _():
             r1_finish(0)
 
-        @pl.when(p == 5)
+        @pl.when(p == 7)
         def _():
             r2_finish(0)
 
     go(r1, 1)
+    for p in (PAIRS - 2, PAIRS - 1):
+        relay(p, True)
 
     level_no = lax.broadcasted_iota(jnp.int32, (8, FAR), 0)
     list_row = lax.broadcasted_iota(jnp.int32, (8, FAR), 1)
@@ -449,6 +528,11 @@
             c.wait_send()
         for c in outs(p):
             c.wait()
+
+        @pl.when((z == 0) | (z == 3))
+        def _():
+            onward(p, False)[0].wait_send()
+            onward(p, True)[0].wait_send()
 
 
 def shards(queries, key_vectors, values, out_grad, far_lists, level_bias):
@@ -472,17 +556,18 @@
             pltpu.VMEM((PAIRS, 2, RIM, PAIR), BF16),
             pltpu.VMEM((PAIRS, 2, RIM, PAIR), BF16),
             pltpu.VMEM((PAIRS, 2, RIM, PAIR), BF16),
-            pltpu.VMEM((2, 4, 4, 16, WIDTH), BF16),
-            pltpu.VMEM((2, 4, 4, 16, WIDTH), BF16),
+            pltpu.VMEM((2, 4, 16, WIDTH), BF16),
+            pltpu.VMEM((2, 4, FAR, WIDTH), BF16),
+            pltpu.VMEM((2, 4, FAR, WIDTH), BF16),
+            pltpu.VMEM((2, 4, FAR, WIDTH), BF16),
             pltpu.VMEM((4, 8, WIDTH), F32),
             pltpu.VMEM((16, WIDTH), F32),
-            pltpu.VMEM((2, 4, 4, 16, WIDTH), BF16),
             pltpu.VMEM((2, 4, 16, WIDTH), BF16),
             pltpu.VMEM((2, 4, 16, WIDTH), BF16),
             pltpu.VMEM((4, 8, WIDTH), F32),
             pltpu.VMEM((4, 8, WIDTH), F32),
             pltpu.VMEM((8, WIDTH), F32),
-            pltpu.VMEM((FAR, 4 * BLOCKS), BF16),
+            pltpu.VMEM((2, 4 * FAR, 64), BF16),
             pltpu.VMEM((FAR, 128), F32),
             pltpu.VMEM((4, 8, 128), F32),
             pltpu.VMEM((4, 8, 128), F32),
@@ -491,7 +576,10 @@
             pltpu.VMEM((2, LIST, LEAF), F32),
             pltpu.VMEM((2, LIST, LEAF), BF16),
             pltpu.VMEM((2, LIST, LEAF), BF16),
-            dma((PAIRS, 2, 2)), dma((PAIRS, 2, 2)), dma((PAIRS, 2)), dma((PAIRS, 2)),
+            pltpu.VMEM((PAIRS, RIM, PAIR), BF16),
+            pltpu.VMEM((PAIRS, RIM, PAIR), BF16),
+            dma((PAIRS, 2)), dma((PAIRS, 2)),
+            dma((PAIRS, 2, 2)), dma((PAIRS, 2, 2)), dma((PAIRS, 2, 2)), dma((PAIRS, 2, 2)),
             dma((PAIRS, 4)), dma((PAIRS, 4)),
             dma((3,)), dma((3,)), dma((2, 3)), dma((2, 3)), dma((2, 3)), dma((2, 3)),
             dma((2, 2, 3)), dma((2, 2, 3)), dma((2, 2, 3)), dma((2, 2, 3)), dma((2, 3)), dma((2, 3)),

time: 178 us -> 137 us (0.77)
  Pallas kernels: 166 us -> 124 us
    pallas_call x1, Pallas kernels: 166 us -> 124 us  [shards(): pl.pallas_call(kernel, out_shape=[jax.ShapeDtypeStruct((LEAF, WIDTH), BF1...]
where the time goes in v2:
time: 137 us; the launch traced here: 136 us
  Pallas kernels  124 us (91%)
  local copies, waits for them, and re-layouts  11.3 us (8%)
    pallas_call x1, Pallas kernels, shards(): pl.pallas_call(kernel, out_shape=[jax.ShapeDtypeStruct((LEAF, WIDTH), BF1...  124 us
    unnamed x14, local copies, waits for them, and re-layouts  11.3 us

profile of v2, /device:TPU:1, one launch (start us, length us, event | category | flops | bytes accessed | tf_op | source)
XLA Modules:
  0.0 135.8 jit_solution(9514853837867728258)
XLA Ops:
  0.6 1.4 %copy.11 = s32[1,64,12]{2,1,0:T(8,128)} copy(s32[1,64,12]{1,0,2:T(1,128)} %param.10) | data formatting | bytes 6144 | tf_op args[4]
  2.0 123.8 %shard_map.101 = (bf16[512,2048]{1,0:T(8,128)(2,1)}, bf16[512,2048]{1,0:T(8,128)(2,1)}, bf16[512,2048]{1,0:T(8,128)(2,1)}, bf16[512,2048]{1,0:T(8,128)(2,1)}, f32[3,16]{1,0:T(4,128)}) custom-call(bf16[512,2048]{1,0:T(8,128)(2,1)} %bitcast.14, bf16[512,2048]{1,0:T(8,128)(2,1)} %bitcast.15, bf16[512,2048]{1,0:T(8,128)(2,1)} %bitcast.16, ...), custom_call_target="tpu_custom_call" | custom-call | flops 13287555072 | bytes 16777216 | tf_op jit(solution)/shard_map/pallas_call | solution.py:542
  125.9 0.0 copy-start.2
  125.9 3.3 %copy.17 = bf16[1,512,2048]{2,1,0:T(8,128)(2,1)} copy(bf16[1,512,2048]{2,1,0:T(8,128)(2,1)} %bitcast.12) | data formatting | bytes 4194304
  129.2 0.0 copy-done.2
  129.2 0.0 copy-start.1
  129.2 1.3 copy.18
  130.5 1.0 copy-done.1
  131.5 0.0 copy-start
  131.5 1.3 copy.19
  132.9 1.0 copy-done
  133.9 0.0 copy-start.3
  133.9 1.3 copy.20
  135.2 0.0 copy-done.3
  135.2 0.6 copy.21
Async XLA Ops:
  125.9 3.3 %copy-start.2 = (bf16[512,2048]{1,0:T(8,128)(2,1)S(1)}, bf16[512,2048]{1,0:T(8,128)(2,1)}, u32[]{:S(2)}) copy-start(bf16[512,2048]{1,0:T(8,128)(2,1)} %get-tuple-element.11) | copy-start | bytes 6291460
  129.2 2.3 %copy-start.1 = (bf16[512,2048]{1,0:T(8,128)(2,1)S(1)}, bf16[512,2048]{1,0:T(8,128)(2,1)}, u32[]{:S(2)}) copy-start(bf16[512,2048]{1,0:T(8,128)(2,1)} %get-tuple-element.12) | copy-start | bytes 6291460
  131.5 2.3 %copy-start = (bf16[512,2048]{1,0:T(8,128)(2,1)S(1)}, bf16[512,2048]{1,0:T(8,128)(2,1)}, u32[]{:S(2)}) copy-start(bf16[512,2048]{1,0:T(8,128)(2,1)} %get-tuple-element.13) | copy-start | bytes 6291460
  133.9 1.3 copy-start.3

commit v3 on v2

v3 whole, which is shorter than its diff:
```python
import functools
import math

import jax
import jax.numpy as jnp
from jax import lax
from jax.experimental import pallas as pl
from jax.experimental.pallas import tpu as pltpu
from jax.sharding import PartitionSpec as P

HEADS = 16
DIM = 128
WIDTH = HEADS * DIM
LEAF = 512
RIM = 256
BLOCKS = 64
PAIRS = 8
PAIR = 2 * DIM
NEAR = LEAF + 2 * RIM
FAR = 32
LIST = NEAR + FAR
SCALE = 1.0 / math.sqrt(DIM)
LOG2E = math.log2(math.e)
BIG = 1e30
MESH = pl.DeviceIdType.MESH
F32 = jnp.float32
BF16 = jnp.bfloat16
PARTS = ((0, 6 * PAIR), (6 * PAIR, 2 * PAIR))

DIRECT, SPLIT, RELAY = (False, False), (False, True), (True, True)
FWD_ROUTE = (SPLIT,) * PAIRS
BWD_ROUTE = (SPLIT,) * PAIRS
PROLOGUE = ((("f", 0),), (), tuple(("f", p) for p in range(1, PAIRS)), (("rf", 0),), (("rf", 1), ("rf", 2)))
BEFORE = ((),) * PAIRS
AFTER = (
    (("b", 0), ("rf", 3)),
    (("b", 1), ("rf", 4)),
    (("b", 2), ("rf", 5), ("rb", 0)),
    (("b", 3), ("rf", 6), ("rb", 1)),
    (("b", 4), ("rf", 7), ("rb", 2)),
    (("b", 5), ("rb", 3), ("x", 0)),
    (("b", 6), ("rb", 4)),
    (("b", 7), ("rb", 5), ("y", 0)),
)
TAIL = (
    ("x", 1), ("l", 0), ("w", 0), ("y", 1), ("l", 1), ("v", 0), ("rb", 6), ("s", 0), ("s", 1), ("s", 2), ("s", 3),
    ("w", 1), ("l", 2), ("rb", 7), ("s", 4), ("s", 5), ("l", 3), ("v", 1), ("s", 6), ("s", 7),
)

NT = (((1,), (1,)), ((), ()))
TN = (((0,), (0,)), ((), ()))
NN = (((1,), (0,)), ((), ()))

CHUNKS = ((0, 256), (256, 256), (512, 256), (768, 256), (1024, FAR))


def dot(a, b, dims=NN):
    return lax.dot_general(a, b, dims, preferred_element_type=F32)


def selector(lists_ref, reader, block):
    shape = (FAR, 64)
    row = lax.broadcasted_iota(jnp.int32, shape, 0)
    col = lax.broadcasted_iota(jnp.int32, shape, 1)
    wanted = jnp.full(shape, -1, jnp.int32)
    first = 0
    for level, count in enumerate((4, 2, 1)):
        for slot in range(4):
            listed = lists_ref[level * 4 + slot, 0, reader]
            wanted = jnp.where((row >= first) & (row < first + count), listed, wanted)
            first += count
    part = col & 3
    one = (row < 16) & (part == (row & 3))
    two = (row >= 16) & (row < 24) & ((part >> 1) == (row & 1))
    share = jnp.where(one, 1.0, 0.0) + jnp.where(two, 0.5, 0.0) + jnp.where(row >= 24, 0.25, 0.0)
    return jnp.where(wanted == block, share, 0.0).astype(BF16)


def kernel(
    q_hbm, k_hbm, v_hbm, g_hbm, lists_ref, bias_ref,
    o_ref, dq_ref, dk_ref, dv_ref, level_ref,
    kx, vx, qx, gx, own, to_down, to_up, from_up, from_down,
    table, chosen, listed, dlisted, zbuf, col32, r2s, r2b, r3s, r3b, far_grad,
    sel_ref, lvl, lvz, lvx, lvy, lvc, s_ref, w_ref, d_ref,
    fwd_relay, bwd_relay, relay_send, relay_recv,
    fwd_send, fwd_recv, bwd_send, bwd_recv, in_sem,
    z_send, z_recv, a1_send, a1_recv, a2_send, a2_recv,
    r1_send, r1_recv, r2_send, r2_recv, r3_send, r3_recv,
    l_send, l_recv, c_send, c_recv,
):
    me = lax.axis_index("seq")
    core = lax.axis_index("batch")
    z = lax.rem(me, 4)
    x = lax.rem(lax.div(me, 4), 4)
    y = lax.div(me, 16)
    up = lax.rem(me + 1, BLOCKS)
    down = lax.rem(me + BLOCKS - 1, BLOCKS)
    next_z = lax.rem(me + 4, BLOCKS)
    last_z = lax.rem(me + BLOCKS - 4, BLOCKS)

    def ahead(c, d):
        return lax.rem(c + d, 4)

    def behind(c, d):
        return lax.rem(c + 4 - d, 4)

    def at_y(c):
        return c * 16 + x * 4 + z

    def at_x(c):
        return y * 16 + c * 4 + z

    def at_z(c):
        return y * 16 + x * 4 + c

    def remote(src, dst, send, recv, to):
        return pltpu.make_async_remote_copy(
            src_ref=src, dst_ref=dst, send_sem=send, recv_sem=recv,
            device_id={"seq": to}, device_id_type=MESH,
        )

    barrier = pltpu.get_barrier_semaphore()
    partners = [up, down, next_z, last_z]
    for d in (1, 2, 3):
        partners += [at_z(ahead(z, d)), at_x(ahead(x, d)), at_y(ahead(y, d))]
    for to in partners:
        pl.semaphore_signal(barrier, inc=1, device_id={"seq": to}, device_id_type=MESH)
    pl.semaphore_signal(barrier, inc=1, device_id={"batch": 1 - core}, device_id_type=MESH)

    def cols(p):
        return pl.ds(pl.multiple_of(p * PAIR, PAIR), PAIR)

    def load(p):
        return [
            pltpu.make_async_copy(k_hbm.at[:, cols(p)], kx.at[p, pl.ds(RIM, LEAF), :], in_sem.at[p, 0]),
            pltpu.make_async_copy(v_hbm.at[:, cols(p)], vx.at[p, pl.ds(RIM, LEAF), :], in_sem.at[p, 1]),
            pltpu.make_async_copy(q_hbm.at[:, cols(p)], qx.at[p], in_sem.at[p, 2]),
            pltpu.make_async_copy(g_hbm.at[:, cols(p)], gx.at[p], in_sem.at[p, 3]),
        ]

    low_rim, high_rim = pl.ds(0, RIM), pl.ds(RIM + LEAF, RIM)

    def rims(p):
        lower, upper = pl.ds(0, RIM), pl.ds(RIM, RIM)
        found = []
        for i, (src, dst) in enumerate(((k_hbm, kx), (v_hbm, vx))):
            found.append(remote(src.at[upper, cols(p)], dst.at[p, low_rim, :], fwd_send.at[p, i, 0], fwd_recv.at[p, i, 0], up))
            found.append(remote(src.at[lower, cols(p)], dst.at[p, high_rim, :], fwd_send.at[p, i, 1], fwd_recv.at[p, i, 1], down))
        return found

    def back(p):
        found = []
        for i in (0, 1):
            found.append(remote(to_up.at[p, i], from_down.at[p, i], bwd_send.at[p, i, 0], bwd_recv.at[p, i, 0], up))
            found.append(remote(to_down.at[p, i], from_up.at[p, i], bwd_send.at[p, i, 1], bwd_recv.at[p, i, 1], down))
        return found

    def detour(p, i, backward):
        if backward:
            up_part, down_part, held, send = to_up.at[p, i], to_down.at[p, i], bwd_relay.at[p, i], bwd_send
        else:
            src = (k_hbm, v_hbm)[i]
            up_part, down_part = src.at[pl.ds(RIM, RIM), cols(p)], src.at[pl.ds(0, RIM), cols(p)]
            held, send = fwd_relay.at[p, i], fwd_send
        recv = relay_recv.at[backward, p, i]
        return (remote(up_part, held, send.at[p, i, 0], recv, at_z(0)),
                remote(down_part, held, send.at[p, i, 1], recv, at_z(3)))

    def onward(p, i, backward):
        send = relay_send.at[backward, p, i]
        if backward:
            held, recv, ups, downs = bwd_relay.at[p, i], bwd_recv, from_down.at[p, i], from_up.at[p, i]
        else:
            dst = (kx, vx)[i]
            held, recv, ups, downs = fwd_relay.at[p, i], fwd_recv, dst.at[p, low_rim, :], dst.at[p, high_rim, :]
        return (remote(held, ups, send, recv.at[p, i, 0], next_z),
                remote(held, downs, send, recv.at[p, i, 1], last_z))

    def start_when(condition, copy):
        @pl.when(condition)
        def _():
            copy.start()

    def send_out(p, backward):
        copies = back(p) if backward else rims(p)
        for i in (0, 1):
            part_up, part_down = copies[2 * i : 2 * i + 2]
            if (FWD_ROUTE, BWD_ROUTE)[backward][p][i]:
                far_up, far_down = detour(p, i, backward)
                start_when(z != 3, part_up)
                start_when(z == 3, far_up)
                start_when(z != 0, part_down)
                start_when(z == 0, far_down)
            else:
                part_up.start()
                part_down.start()

    def relay(p, backward):
        for i in (0, 1):
            if (FWD_ROUTE, BWD_ROUTE)[backward][p][i]:
                for place, came, on in zip((0, 3), detour(p, i, backward), onward(p, i, backward)):
                    @pl.when(z == place)
                    def _():
                        came.wait_recv()
                        on.start()

    def part_lanes(part):
        return pl.ds(*PARTS[part])

    def r1(part, d):
        n = part_lanes(part)
        yp, xp = ahead(y, d), ahead(x, d)
        return [
            remote(dlisted.at[0, y, :, n], dlisted.at[0, y, :, n], r1_send.at[part, 0, d - 1], r1_recv.at[part, 0, d - 1], at_y(yp)),
            remote(dlisted.at[1, x, :, n], dlisted.at[1, x, :, n], r1_send.at[part, 1, d - 1], r1_recv.at[part, 1, d - 1], at_x(xp)),
        ]

    def r2(part, d):
        n = part_lanes(part)
        yp, xp = ahead(y, d), ahead(x, d)
        return [
            remote(r2s.at[0, xp, :, n], r2b.at[0, x, :, n], r2_send.at[part, 0, d - 1], r2_recv.at[part, 0, d - 1], at_x(xp)),
            remote(r2s.at[1, yp, :, n], r2b.at[1, y, :, n], r2_send.at[part, 1, d - 1], r2_recv.at[part, 1, d - 1], at_y(yp)),
        ]

    def r3(part, d):
        n = part_lanes(part)
        zp = ahead(z, d)
        return [remote(r3s.at[zp, :, n], r3b.at[z, :, n], r3_send.at[part, d - 1], r3_recv.at[part, d - 1], at_z(zp))]

    def go(step, part):
        for d in (1, 2, 3):
            for c in step(part, d):
                c.start()

    def got(step, part):
        for d in (1, 2, 3):
            for c in step(part, d):
                c.wait_recv()

    def r1_finish(part):
        got(r1, part)
        for i in (0, 1):
            for first in range(0, PARTS[part][1], 512):
                n = pl.ds(PARTS[part][0] + first, 512)
                terms = dot(sel_ref[i], dlisted[i, :, :, n].reshape(4 * FAR, 512), TN)
                r2s[i, :, :, n] = terms.astype(BF16).reshape(4, 16, 512)
        go(r2, part)

    def r2_finish(part):
        n = part_lanes(part)
        got(r2, part)
        for j, c in enumerate((x, y)):
            total = r2s[j, c, :, n].astype(F32)
            for d in (1, 2, 3):
                total = total + r2b[j, behind(c, d), :, n].astype(F32)
            col32[:, n] = total
            for i in range(4):
                r3s[i, 4 * j : 4 * j + 4, n] = col32[4 * i : 4 * i + 4, n]
        go(r3, part)

    def r3_finish(part):
        n = part_lanes(part)
        got(r3, part)
        total = r3s[z, :, n]
        for d in (1, 2, 3):
            total = total + r3b[behind(z, d), :, n]
        far_grad[:, n] = total * (1.0 / 128)

    swap = pltpu.make_async_remote_copy(
        src_ref=lvc.at[core], dst_ref=lvc.at[core], send_sem=c_send, recv_sem=c_recv,
        device_id={"batch": 1 - core}, device_id_type=MESH)

    def level_copy(buf, c, step, d, to):
        return remote(buf.at[c], buf.at[c], l_send.at[step, d - 1], l_recv.at[step, d - 1], to)

    def level_steps(step):
        buf, c, at = ((lvy, y, at_y), (lvx, x, at_x), (lvz, z, at_z))[step]
        return [level_copy(buf, c, step, d, at(ahead(c, d))) for d in (1, 2, 3)]

    def level_sum(step):
        for c in level_steps(step):
            c.wait_recv()
        buf = (lvy, lvx, lvz)[step]
        return (buf[0] + buf[1]) + (buf[2] + buf[3])

    def level_step(n):
        if n == 0:
            level_no = lax.broadcasted_iota(jnp.int32, (8, FAR), 0)
            list_row = lax.broadcasted_iota(jnp.int32, (8, FAR), 1)
            level_of = jnp.where(list_row < 16, 0, jnp.where(list_row < 24, 1, jnp.where(list_row < 28, 2, 9)))
            pick = jnp.where(level_no == level_of, 1.0, 0.0).astype(F32)
            lvy[y] = lax.dot_general(pick, lvl[...], NN, precision=lax.Precision.HIGHEST, preferred_element_type=F32)
        else:
            buf, c = ((lvx, x), (lvz, z), (lvc, core))[n - 1]
            buf[c] = level_sum(n - 1)
        for c in level_steps(n) if n < 3 else [swap]:
            c.start()

    def settle(p):
        for c in back(p):
            c.wait_recv()
        for i, dst in enumerate((dk_ref, dv_ref)):
            for r in range(4):
                tokens = pl.ds(128 * r, 128)
                total = own[p, i, tokens, :] + far_grad[4 * i + r : 4 * i + r + 1, cols(p)]
                if r < 2:
                    total = total + from_down[p, i, tokens, :].astype(F32)
                else:
                    total = total + from_up[p, i, pl.ds(128 * (r - 2), 128), :].astype(F32)
                dst[tokens, cols(p)] = total.astype(BF16)

    def act(steps):
        for kind, n in steps:
            if kind in ("f", "b"):
                send_out(n, ("f", "b").index(kind))
            elif kind in ("rf", "rb"):
                relay(n, ("rf", "rb").index(kind))
            elif kind == "x":
                go(r1, n)
            else:
                {"y": r1_finish, "w": r2_finish, "v": r3_finish, "s": settle, "l": level_step}[kind](n)

    @pl.loop(0, PAIRS)
    def _(p):
        for c in load(p)[:2]:
            c.start()

    @pl.loop(0, PAIRS)
    def _(p):
        for c in load(p)[2:]:
            c.start()

    pl.semaphore_wait(barrier, 14)
    act(PROLOGUE[0])

    col_block = lax.broadcasted_iota(jnp.int32, (FAR, 64), 1) // 4
    key_block = y * 16 + col_block
    value_block = (col_block // 4) * 16 + x * 4 + (col_block & 3)
    for i in range(4):
        sel_ref[0, i * FAR : (i + 1) * FAR, :] = selector(lists_ref, at_y(i), key_block)
        sel_ref[1, i * FAR : (i + 1) * FAR, :] = selector(lists_ref, at_x(i), value_block)

    pool_row = lax.broadcasted_iota(jnp.int32, (8, LEAF), 0)
    pool_tok = lax.broadcasted_iota(jnp.int32, (8, LEAF), 1) // 128
    pool_k = jnp.where(pool_tok == pool_row, 1.0 / 128, 0.0).astype(BF16)
    pool_v = jnp.where(pool_tok + 4 == pool_row, 1.0 / 128, 0.0).astype(BF16)

    @pl.loop(0, PAIRS)
    def _(p):
        for c in load(p)[:2]:
            c.wait()
        mine = pl.ds(RIM, LEAF)
        zbuf[z, :, cols(p)] = dot(pool_k, kx[p, mine, :]) + dot(pool_v, vx[p, mine, :])

    def gather_z(d):
        return remote(zbuf.at[z], zbuf.at[z], z_send.at[d - 1], z_recv.at[d - 1], at_z(ahead(z, d)))

    for d in (1, 2, 3):
        gather_z(d).start()
    act(PROLOGUE[1])
    for d in (1, 2, 3):
        gather_z(d).wait_recv()
    for i in (0, 1):
        for c in range(4):
            col32[4 * c : 4 * c + 4, :] = zbuf[c, 4 * i : 4 * i + 4, :]
        table[i, (x, y)[i]] = col32[...].astype(BF16)

    def gather_one(d):
        return [
            remote(table.at[0, x], table.at[0, x], a1_send.at[0, d - 1], a1_recv.at[0, d - 1], at_x(ahead(x, d))),
            remote(table.at[1, y], table.at[1, y], a1_send.at[1, d - 1], a1_recv.at[1, d - 1], at_y(ahead(y, d))),
        ]

    def gather_two(d):
        yp, xp = ahead(y, d), ahead(x, d)
        return [
            remote(chosen.at[0, yp], listed.at[0, y], a2_send.at[0, d - 1], a2_recv.at[0, d - 1], at_y(yp)),
            remote(chosen.at[1, xp], listed.at[1, x], a2_send.at[1, d - 1], a2_recv.at[1, d - 1], at_x(xp)),
        ]

    for d in (1, 2, 3):
        for c in gather_one(d):
            c.start()
    act(PROLOGUE[2])
    for d in (1, 2, 3):
        for c in gather_one(d):
            c.wait_recv()
    for i in (0, 1):
        for n in range(0, WIDTH, 512):
            rows = table[i, :, :, n : n + 512].reshape(64, 512)
            chosen[i, :, :, n : n + 512] = dot(sel_ref[i], rows).astype(BF16).reshape(4, FAR, 512)
    for d in (1, 2, 3):
        for c in gather_two(d):
            c.start()
    listed[0, y] = chosen[0, y]
    listed[1, x] = chosen[1, x]

    act(PROLOGUE[3])
    for d in (1, 2, 3):
        for c in gather_two(d):
            c.wait_recv()
    act(PROLOGUE[4])

    lane_sel = lax.broadcasted_iota(jnp.int32, (FAR, 128), 1)
    far_row = lax.broadcasted_iota(jnp.int32, (FAR, 1), 0)
    lvl[...] = jnp.zeros_like(lvl)
    low_gap = jnp.where(me == 0, BIG, 0.0).astype(F32)
    high_gap = jnp.where(me == BLOCKS - 1, BIG, 0.0).astype(F32)
    gaps = (low_gap, None, None, high_gap, None)
    factor = SCALE * LOG2E

    def head(p, h):
        lanes = slice(h * DIM, h * DIM + DIM)
        head_no = 2 * p + h
        head_lanes = pl.ds(pl.multiple_of(head_no * DIM, DIM), DIM)
        bias = jnp.where(
            far_row < 16, bias_ref[0, head_no] + math.log(128),
            jnp.where(far_row < 24, bias_ref[1, head_no] + math.log(256),
                      jnp.where(far_row < 28, bias_ref[2, head_no] + math.log(512), -BIG)))
        bias = bias * LOG2E
        query = qx[p, :, lanes]
        grad = gx[p, :, lanes]
        top = None
        for (first, rows), gap in zip(CHUNKS, gaps):
            s = dot(kx[p, first : first + rows, lanes], query, NT) * factor
            if rows == FAR:
                s = s + bias
            s_ref[h, first : first + rows, :] = s
            peak = jnp.max(s, axis=0, keepdims=True)
            if gap is not None:
                peak = peak - gap
            top = peak if top is None else jnp.maximum(top, peak)
        total = jnp.zeros((1, LEAF), F32)
        for (first, rows), gap in zip(CHUNKS, gaps):
            base = top if gap is None else top + gap
            e = jnp.exp2(s_ref[h, first : first + rows, :] - base)
            s_ref[h, first : first + rows, :] = e
            total = total + jnp.sum(e, axis=0, keepdims=True)
        inverse = 1.0 / total
        for first, rows in CHUNKS:
            w_ref[h, first : first + rows, :] = (s_ref[h, first : first + rows, :] * inverse).astype(BF16)
        out = dot(vx[p, :, lanes], w_ref[h], TN).T.astype(BF16)
        o_ref[:, head_lanes] = out
        ones = jnp.ones((8, DIM), F32)
        row_dot = lax.dot_general(
            ones, out.astype(F32) * grad.astype(F32), NT,
            precision=lax.Precision.HIGHEST, preferred_element_type=F32)[0:1, :]
        for first, rows in CHUNKS:
            dw = dot(vx[p, first : first + rows, lanes], grad, NT)
            ds = s_ref[h, first : first + rows, :] * inverse * (dw - row_dot)
            d_ref[h, first : first + rows, :] = ds.astype(BF16)
            if rows == FAR:
                sums = jnp.sum(ds, axis=1, keepdims=True)
                lvl[...] += jnp.where(lane_sel == head_no, sums, 0.0)
        dq_ref[:, head_lanes] = (dot(kx[p, :, lanes], d_ref[h], TN) * SCALE).T.astype(BF16)
        dk = dot(d_ref[h], query) * SCALE
        dv = dot(w_ref[h], grad)
        for i, term in enumerate((dk, dv)):
            to_down[p, i, :, lanes] = term[:RIM].astype(BF16)
            own[p, i, :, lanes] = term[RIM : RIM + LEAF]
            to_up[p, i, :, lanes] = term[RIM + LEAF : NEAR].astype(BF16)
        return dk[NEAR:], dv[NEAR:]

    @pl.loop(0, PAIRS)
    def _(p):
        for i, dst in enumerate((kx, vx)):
            rows = listed[i, :, :, cols(p)].astype(F32)
            dst[p, NEAR:LIST, :] = ((rows[0] + rows[1]) + (rows[2] + rows[3])).astype(BF16)
        for c in load(p)[2:]:
            c.wait()
        for c in rims(p):
            c.wait_recv()

        def at_step(k, steps):
            if steps:
                @pl.when(p == k)
                def _():
                    act(steps)

        for k in range(PAIRS):
            at_step(k, BEFORE[k])
        first = head(p, 0)
        second = head(p, 1)
        for i, slot in ((0, y), (1, x)):
            dlisted[i, slot, :, cols(p)] = jnp.concatenate([first[i], second[i]], axis=1).astype(BF16)

        for k in range(PAIRS):
            at_step(k, AFTER[k])

    act(TAIL)

    swap.wait_recv()
    level_ref[...] = ((lvc[0] + lvc[1]) * (1.0 / math.sqrt(2 * BLOCKS * LEAF)))[0:3, 0:HEADS]

    swap.wait_send()
    for step in range(3):
        for c in level_steps(step):
            c.wait_send()
    for d in (1, 2, 3):
        gather_z(d).wait_send()
        for c in gather_one(d) + gather_two(d):
            c.wait_send()
        for part in (0, 1):
            for c in r1(part, d) + r2(part, d) + r3(part, d):
                c.wait_send()

    @pl.loop(0, PAIRS)
    def _(p):
        for c in rims(p) + back(p):
            c.wait_send()

    @pl.when((z == 0) | (z == 3))
    def _():
        for backward in (0, 1):
            for p in range(PAIRS):
                for i in (0, 1):
                    if (FWD_ROUTE, BWD_ROUTE)[backward][p][i]:
                        onward(p, i, backward)[0].wait_send()


def shards(queries, key_vectors, values, out_grad, far_lists, level_bias):
    any_spec = pl.BlockSpec(memory_space=pl.ANY)
    smem = pl.BlockSpec(memory_space=pltpu.SMEM)
    dma = pltpu.SemaphoreType.DMA
    outs = pl.pallas_call(
        kernel,
        out_shape=[pltpu.VMEM((LEAF, WIDTH), BF16)] * 4 + [pltpu.VMEM((3, HEADS), F32)],
        in_specs=[any_spec] * 4 + [smem] * 2,
        out_specs=[pl.BlockSpec(memory_space=pltpu.VMEM)] * 4 + [pl.BlockSpec(memory_space=pltpu.VMEM)],
        scratch_shapes=[
            pltpu.VMEM((PAIRS, LIST, PAIR), BF16),
            pltpu.VMEM((PAIRS, LIST, PAIR), BF16),
            pltpu.VMEM((PAIRS, LEAF, PAIR), BF16),
            pltpu.VMEM((PAIRS, LEAF, PAIR), BF16),
            pltpu.VMEM((PAIRS, 2, LEAF, PAIR), F32),
            pltpu.VMEM((PAIRS, 2, RIM, PAIR), BF16),
            pltpu.VMEM((PAIRS, 2, RIM, PAIR), BF16),
            pltpu.VMEM((PAIRS, 2, RIM, PAIR), BF16),
            pltpu.VMEM((PAIRS, 2, RIM, PAIR), BF16),
            pltpu.VMEM((2, 4, 16, WIDTH), BF16),
            pltpu.VMEM((2, 4, FAR, WIDTH), BF16),
            pltpu.VMEM((2, 4, FAR, WIDTH), BF16),
            pltpu.VMEM((2, 4, FAR, WIDTH), BF16),
            pltpu.VMEM((4, 8, WIDTH), F32),
            pltpu.VMEM((16, WIDTH), F32),
            pltpu.VMEM((2, 4, 16, WIDTH), BF16),
            pltpu.VMEM((2, 4, 16, WIDTH), BF16),
            pltpu.VMEM((4, 8, WIDTH), F32),
            pltpu.VMEM((4, 8, WIDTH), F32),
            pltpu.VMEM((8, WIDTH), F32),
            pltpu.VMEM((2, 4 * FAR, 64), BF16),
            pltpu.VMEM((FAR, 128), F32),
            pltpu.VMEM((4, 8, 128), F32),
            pltpu.VMEM((4, 8, 128), F32),
            pltpu.VMEM((4, 8, 128), F32),
            pltpu.VMEM((2, 8, 128), F32),
            pltpu.VMEM((2, LIST, LEAF), F32),
            pltpu.VMEM((2, LIST, LEAF), BF16),
            pltpu.VMEM((2, LIST, LEAF), BF16),
            pltpu.VMEM((PAIRS, 2, RIM, PAIR), BF16),
            pltpu.VMEM((PAIRS, 2, RIM, PAIR), BF16),
            dma((2, PAIRS, 2)), dma((2, PAIRS, 2)),
            dma((PAIRS, 2, 2)), dma((PAIRS, 2, 2)), dma((PAIRS, 2, 2)), dma((PAIRS, 2, 2)),
            dma((PAIRS, 4)),
            dma((3,)), dma((3,)), dma((2, 3)), dma((2, 3)), dma((2, 3)), dma((2, 3)),
            dma((2, 2, 3)), dma((2, 2, 3)), dma((2, 2, 3)), dma((2, 2, 3)), dma((2, 3)), dma((2, 3)),
            dma((3, 3)), dma((3, 3)), dma, dma,
        ],
        compiler_params=pltpu.CompilerParams(
            collective_id=0, has_side_effects=True, vmem_limit_bytes=54 * 1024 * 1024),
        cost_estimate=pl.CostEstimate(
            flops=12 * HEADS * LEAF * LIST * DIM, bytes_accessed=8 * LEAF * WIDTH * 2,
            transcendentals=HEADS * LEAF * LIST),
    )(queries[0], key_vectors[0], values[0], out_grad[0], far_lists.transpose(2, 0, 1), level_bias)
    return tuple(o[None] for o in outs[:4]) + (outs[4],)


def solution(mesh):
    token = P("batch", "seq", None)
    return jax.shard_map(
        shards,
        mesh=mesh,
        in_specs=(token, token, token, token, P("batch", None, None), P()),
        out_specs=(token, token, token, token, P()),
        check_vma=False,
    )
```

time: 137 us -> 127 us (0.927)
  local copies, waits for them, and re-layouts: 11.3 us -> 5.85 us
  Pallas kernels: 124 us -> 120 us
    unnamed x14 -> x5, local copies, waits for them, and re-layouts: 11.3 us -> 5.85 us
    pallas_call x1, Pallas kernels: 124 us -> 120 us  [shards(): pl.pallas_call(kernel, out_shape=[pltpu.VMEM((LEAF, WIDTH), BF16)] * 4 +...]
where the time goes in v3:
time: 127 us
  Pallas kernels  120 us (94%)
  local copies, waits for them, and re-layouts  5.85 us (5%)
    pallas_call x1, Pallas kernels, shards(): pl.pallas_call(kernel, out_shape=[pltpu.VMEM((LEAF, WIDTH), BF16)] * 4 +...  120 us
    unnamed x5, local copies, waits for them, and re-layouts  5.85 us

profile of v3, /device:TPU:1, one launch (start us, length us, event | category | flops | bytes accessed | tf_op | source)
XLA Modules:
  0.0 126.7 jit_solution(4201245561585378121)
XLA Ops:
  0.6 120.2 %shard_map.101 = (bf16[512,2048]{1,0:T(8,128)(2,1)S(1)}, bf16[512,2048]{1,0:T(8,128)(2,1)S(1)}, bf16[512,2048]{1,0:T(8,128)(2,1)S(1)}, bf16[512,2048]{1,0:T(8,128)(2,1)S(1)}, f32[3,16]{1,0:T(4,128)S(1)}) custom-call(bf16[512,2048]{1,0:T(8,128)(2,1)} %bitcast.13, bf16[512,2048]{1,0:T(8,128)(2,1)} %bitcast.14, bf16[512,2048]{1,0:T(8,128)(2,1)} %bitcast.15, ...), custom_call_target="tpu_custom_call" | custom-call | flops 13287555072 | bytes 16777216 | tf_op jit(solution)/shard_map/pallas_call | solution.py:526
  120.9 1.3 %copy.16 = bf16[1,512,2048]{2,1,0:T(8,128)(2,1)} copy(bf16[1,512,2048]{2,1,0:T(8,128)(2,1)S(1)} %bitcast.12) | data formatting | bytes 4194304
  122.2 1.3 %copy.17 = bf16[1,512,2048]{2,1,0:T(8,128)(2,1)} copy(bf16[1,512,2048]{2,1,0:T(8,128)(2,1)S(1)} %bitcast.11) | data formatting | bytes 4194304
  123.5 0.6 copy.20
  124.1 1.3 %copy.18 = bf16[1,512,2048]{2,1,0:T(8,128)(2,1)} copy(bf16[1,512,2048]{2,1,0:T(8,128)(2,1)S(1)} %bitcast.10) | data formatting | bytes 4194304
  125.4 1.3 %copy.19 = bf16[1,512,2048]{2,1,0:T(8,128)(2,1)} copy(bf16[1,512,2048]{2,1,0:T(8,128)(2,1)S(1)} %bitcast.9) | data formatting | bytes 4194304

commit v4 on v3

--- a/solution.py
+++ b/solution.py
@@ -30,20 +30,20 @@
 DIRECT, SPLIT, RELAY = (False, False), (False, True), (True, True)
 FWD_ROUTE = (SPLIT,) * PAIRS
 BWD_ROUTE = (SPLIT,) * PAIRS
-PROLOGUE = ((("f", 0),), (), tuple(("f", p) for p in range(1, PAIRS)), (("rf", 0),), (("rf", 1), ("rf", 2)))
+PROLOGUE = ((("f", 0),), (("f", 1),), tuple(("f", p) for p in range(2, PAIRS)), (("rf", 0),), (("rf", 1), ("rf", 2), ("rf", 3)))
 BEFORE = ((),) * PAIRS
 AFTER = (
-    (("b", 0), ("rf", 3)),
-    (("b", 1), ("rf", 4)),
-    (("b", 2), ("rf", 5), ("rb", 0)),
-    (("b", 3), ("rf", 6), ("rb", 1)),
-    (("b", 4), ("rf", 7), ("rb", 2)),
-    (("b", 5), ("rb", 3), ("x", 0)),
-    (("b", 6), ("rb", 4)),
-    (("b", 7), ("rb", 5), ("y", 0)),
+    (("b", 0), ("rf", 4)),
+    (("b", 1), ("rf", 5)),
+    (("b", 2), ("rf", 6)),
+    (("b", 3), ("rf", 7), ("rb", 0)),
+    (("b", 4), ("rb", 1)),
+    (("b", 5), ("rb", 2), ("x", 0)),
+    (("b", 6), ("rb", 3)),
+    (("b", 7), ("rb", 4), ("y", 0)),
 )
 TAIL = (
-    ("x", 1), ("l", 0), ("w", 0), ("y", 1), ("l", 1), ("v", 0), ("rb", 6), ("s", 0), ("s", 1), ("s", 2), ("s", 3),
+    ("x", 1), ("l", 0), ("w", 0), ("rb", 5), ("y", 1), ("l", 1), ("v", 0), ("rb", 6), ("s", 0), ("s", 1), ("s", 2), ("s", 3),
     ("w", 1), ("l", 2), ("rb", 7), ("s", 4), ("s", 5), ("l", 3), ("v", 1), ("s", 6), ("s", 7),
 )
 

time: 127 us -> 123 us (0.969)
  Pallas kernels: 120 us -> 116 us
    pallas_call x1, Pallas kernels: 120 us -> 116 us  [shards(): pl.pallas_call(kernel, out_shape=[pltpu.VMEM((LEAF, WIDTH), BF16)] * 4 +...]
where the time goes in v4:
time: 123 us
  Pallas kernels  116 us (94%)
  local copies, waits for them, and re-layouts  5.85 us (5%)
    pallas_call x1, Pallas kernels, shards(): pl.pallas_call(kernel, out_shape=[pltpu.VMEM((LEAF, WIDTH), BF16)] * 4 +...  116 us
    unnamed x5, local copies, waits for them, and re-layouts  5.85 us

profile of v4, /device:TPU:1, one launch (start us, length us, event | category | flops | bytes accessed | tf_op | source)
XLA Modules:
  0.0 123.0 jit_solution(7981178601697450772)
XLA Ops:
  0.6 116.5 %shard_map.101 = (bf16[512,2048]{1,0:T(8,128)(2,1)S(1)}, bf16[512,2048]{1,0:T(8,128)(2,1)S(1)}, bf16[512,2048]{1,0:T(8,128)(2,1)S(1)}, bf16[512,2048]{1,0:T(8,128)(2,1)S(1)}, f32[3,16]{1,0:T(4,128)S(1)}) custom-call(bf16[512,2048]{1,0:T(8,128)(2,1)} %bitcast.13, bf16[512,2048]{1,0:T(8,128)(2,1)} %bitcast.14, bf16[512,2048]{1,0:T(8,128)(2,1)} %bitcast.15, ...), custom_call_target="tpu_custom_call" | custom-call | flops 13287555072 | bytes 16777216 | tf_op jit(solution)/shard_map/pallas_call | solution.py:526
  117.1 1.3 %copy.16 = bf16[1,512,2048]{2,1,0:T(8,128)(2,1)} copy(bf16[1,512,2048]{2,1,0:T(8,128)(2,1)S(1)} %bitcast.12) | data formatting | bytes 4194304
  118.4 1.3 %copy.17 = bf16[1,512,2048]{2,1,0:T(8,128)(2,1)} copy(bf16[1,512,2048]{2,1,0:T(8,128)(2,1)S(1)} %bitcast.11) | data formatting | bytes 4194304
  119.8 0.6 copy.20
  120.3 1.3 %copy.18 = bf16[1,512,2048]{2,1,0:T(8,128)(2,1)} copy(bf16[1,512,2048]{2,1,0:T(8,128)(2,1)S(1)} %bitcast.10) | data formatting | bytes 4194304
  121.6 1.3 %copy.19 = bf16[1,512,2048]{2,1,0:T(8,128)(2,1)} copy(bf16[1,512,2048]{2,1,0:T(8,128)(2,1)S(1)} %bitcast.9) | data formatting | bytes 4194304
